TPU v7x, 256 devices: a whole 4x4x8 slice. The times are simulated.
256 devices in a mesh: section: 8 (over z_hi, core), ctx: 8 (over z_lo, x), tp: 4 (over y).
Axes of the slice: x: 4, y: 4, z: 8 (z_hi: 4, z_lo: 2; z = z_hi * 2 + z_lo), core: 2. Of those that a mesh axis runs over, the one named last changes fastest.
Arguments:
- fwd_input: bfloat16 [8, 1024, 6144], P('section', 'ctx', 'tp'), may hold values from -6 to 6
- grad_out: bfloat16 [8, 1024, 6144], P('section', 'ctx', 'tp'), may hold values from -6 to 6
- w_qkv: bfloat16 [8, 3, 6144, 32, 128], P('section', None, 'tp', 'ctx'), may hold values from -1 to 1
- w_out: bfloat16 [8, 32, 128, 6144], P('section', 'ctx', None, 'tp'), may hold values from -0.5 to 0.5
- saved_qkv: bfloat16 [8, 3, 1024, 32, 128], P('section', None, None, ('ctx', 'tp')), may hold values from -6 to 6
- rand_blocks: int32 [8, 32, 16, 3], P('section', ('ctx', 'tp')), may hold values from 0 to 15
Outputs:
- fwd_next: bfloat16 [8, 1024, 6144], P('section', 'ctx', 'tp')
- grad_prev: bfloat16 [8, 1024, 6144], P('section', 'ctx', 'tp')
Inputs may be any that keep to these rules, and one draw needn't show every extreme that they name: `rand_blocks`: key block indices.
All inputs are finite; a program needn't handle non-finite values.
Results may differ from a plain program's by a relative error of at most 0.025.
Values may be sent and summed in bfloat16 or wider, within the bound.
A program may use at most 128 MiB of HBM per device.

v0:
```python
import math

import jax
import jax.numpy as jnp
from jax import lax
from jax.sharding import PartitionSpec as P

BLOCK = 64
GLOB = 2


def passed_along(block, axis, distance):
    devices = range(lax.axis_size(axis))
    route = [((i - distance) % len(devices), i) for i in devices]
    return lax.ppermute(block, axis, route)


def pattern_lists(rand_rows, num_blocks):
    row_ids = lax.broadcasted_iota(jnp.int32, (num_blocks, 3), 0)
    offsets = lax.broadcasted_iota(jnp.int32, (num_blocks, 3), 1) - 1
    near_blocks = (row_ids + offsets + num_blocks) % num_blocks
    glob_blocks = lax.broadcasted_iota(jnp.int32, (num_blocks, GLOB), 1)
    key_lists = jnp.concatenate([near_blocks, glob_blocks, rand_rows], axis=1)
    list_width = key_lists.shape[1]
    same_block = key_lists[:, :, None] == key_lists[:, None, :]
    lower_slot = lax.broadcasted_iota(
        jnp.int32, (list_width, list_width), 0
    ) > lax.broadcasted_iota(jnp.int32, (list_width, list_width), 1)
    first_seen = jnp.logical_not(jnp.any(jnp.logical_and(same_block, lower_slot[None]), axis=2))
    return (key_lists, first_seen)


def plain_probs(queries, keys_in, scaling):
    raw_scores = jnp.dot(queries, keys_in.T, preferred_element_type=jnp.float32) * scaling
    row_top = jnp.max(raw_scores, axis=-1, keepdims=True)
    row_exp = jnp.exp(raw_scores - row_top)
    return row_exp / jnp.sum(row_exp, axis=-1, keepdims=True)


def block_probs(queries, keys_in, key_lists, first_seen, scaling):
    num_blocks = key_lists.shape[0]
    head_dim = queries.shape[1]
    query_blocks = queries.reshape(num_blocks, BLOCK, head_dim)
    key_sel = keys_in.reshape(num_blocks, BLOCK, head_dim)[key_lists]
    raw_scores = (
        jnp.einsum("ibe,iake->ibak", query_blocks, key_sel, preferred_element_type=jnp.float32)
        * scaling
    )
    raw_scores = jnp.where(first_seen[:, None, :, None], raw_scores, -jnp.inf)
    row_top = jnp.max(raw_scores, axis=(2, 3), keepdims=True)
    row_exp = jnp.exp(raw_scores - row_top)
    return (row_exp / jnp.sum(row_exp, axis=(2, 3), keepdims=True), key_sel)


def forward_blocks(queries, keys_in, vals_in, rand_rows):
    head_dim = queries.shape[1]
    num_blocks = queries.shape[0] // BLOCK
    scaling = 1.0 / math.sqrt(head_dim)
    key_lists, first_seen = pattern_lists(rand_rows, num_blocks)
    attn_probs, key_sel = block_probs(queries, keys_in, key_lists, first_seen, scaling)
    val_sel = vals_in.reshape(num_blocks, BLOCK, head_dim)[key_lists]
    sparse_out = jnp.einsum(
        "ibak,iake->ibe",
        attn_probs.astype(jnp.bfloat16),
        val_sel,
        preferred_element_type=jnp.float32,
    ).reshape(-1, head_dim)
    glob_rows = GLOB * BLOCK
    glob_low = plain_probs(queries[:glob_rows], keys_in, scaling).astype(jnp.bfloat16)
    glob_out = jnp.dot(glob_low, vals_in, preferred_element_type=jnp.float32)
    return jnp.concatenate([glob_out, sparse_out[glob_rows:]], axis=0).astype(jnp.bfloat16)


def backward_blocks(queries, keys_in, vals_in, grad_mix, rand_rows):
    head_dim = queries.shape[1]
    num_blocks = queries.shape[0] // BLOCK
    scaling = 1.0 / math.sqrt(head_dim)
    key_lists, first_seen = pattern_lists(rand_rows, num_blocks)
    attn_probs, key_sel = block_probs(queries, keys_in, key_lists, first_seen, scaling)
    val_sel = vals_in.reshape(num_blocks, BLOCK, head_dim)[key_lists]
    query_blocks = queries.reshape(num_blocks, BLOCK, head_dim)
    grad_blocks = grad_mix.reshape(num_blocks, BLOCK, head_dim)
    keep_rows = lax.broadcasted_iota(jnp.int32, (num_blocks, 1, 1, 1), 0) >= GLOB
    weights_low = jnp.where(keep_rows, attn_probs, 0.0).astype(jnp.bfloat16)
    head_out = jnp.einsum(
        "ibak,iake->ibe", weights_low, val_sel, preferred_element_type=jnp.float32
    ).astype(jnp.bfloat16)
    row_delta = jnp.sum(grad_blocks.astype(jnp.float32) * head_out.astype(jnp.float32), axis=-1)[
        :, :, None, None
    ]
    grad_probs = jnp.einsum(
        "ibe,iake->ibak", grad_blocks, val_sel, preferred_element_type=jnp.float32
    )
    grad_scores = jnp.where(keep_rows, attn_probs * (grad_probs - row_delta), 0.0).astype(
        jnp.bfloat16
    )
    grad_q_sparse = jnp.einsum(
        "ibak,iake->ibe", grad_scores, key_sel, preferred_element_type=jnp.float32
    ).reshape(-1, head_dim)
    grad_k_sel = jnp.einsum(
        "ibak,ibe->iake", grad_scores, query_blocks, preferred_element_type=jnp.float32
    )
    grad_v_sel = jnp.einsum(
        "ibak,ibe->iake", weights_low, grad_blocks, preferred_element_type=jnp.float32
    )
    block_ids = lax.broadcasted_iota(jnp.int32, (num_blocks, key_lists.shape[1], num_blocks), 2)
    spread = jnp.logical_and(key_lists[:, :, None] == block_ids, first_seen[:, :, None]).astype(
        jnp.float32
    )
    grad_k_sparse = jnp.einsum(
        "iaj,iake->jke", spread, grad_k_sel, precision=lax.Precision.HIGHEST
    ).reshape(-1, head_dim)
    grad_v_sparse = jnp.einsum(
        "iaj,iake->jke", spread, grad_v_sel, precision=lax.Precision.HIGHEST
    ).reshape(-1, head_dim)
    glob_rows = GLOB * BLOCK
    glob_query = queries[:glob_rows]
    glob_grad = grad_mix[:glob_rows]
    glob_probs = plain_probs(glob_query, keys_in, scaling)
    glob_low = glob_probs.astype(jnp.bfloat16)
    glob_out = jnp.dot(glob_low, vals_in, preferred_element_type=jnp.float32).astype(jnp.bfloat16)
    glob_delta = jnp.sum(
        glob_grad.astype(jnp.float32) * glob_out.astype(jnp.float32), axis=-1, keepdims=True
    )
    glob_scores = (
        glob_probs
        * (jnp.dot(glob_grad, vals_in.T, preferred_element_type=jnp.float32) - glob_delta)
    ).astype(jnp.bfloat16)
    glob_q = jnp.dot(glob_scores, keys_in, preferred_element_type=jnp.float32)
    grad_q = (jnp.concatenate([glob_q, grad_q_sparse[glob_rows:]], axis=0) * scaling).astype(
        jnp.bfloat16
    )
    grad_k = (
        (grad_k_sparse + jnp.dot(glob_scores.T, glob_query, preferred_element_type=jnp.float32))
        * scaling
    ).astype(jnp.bfloat16)
    grad_v = (
        grad_v_sparse + jnp.dot(glob_low.T, glob_grad, preferred_element_type=jnp.float32)
    ).astype(jnp.bfloat16)
    return (grad_q, grad_k, grad_v)


def pass_on(block_value, steps_by):
    return passed_along(block_value, "section", steps_by)


def per_device(fwd_input, grad_out, w_qkv, w_out, saved_qkv, rand_blocks):
    inputs_now = fwd_input[0]
    grads_now = grad_out[0]
    proj_in = w_qkv[0]
    proj_out = w_out[0]
    stored = saved_qkv[0]
    random_rows = rand_blocks[0]
    all_inputs, all_grads = (
        lax.all_gather(inputs_now, "ctx", axis=0, tiled=True),
        lax.all_gather(grads_now, "ctx", axis=0, tiled=True),
    )
    qkv_part = jnp.einsum("ld,cdhe->clhe", all_inputs, proj_in, preferred_element_type=jnp.float32)
    mix_part = jnp.einsum("ld,hed->lhe", all_grads, proj_out, preferred_element_type=jnp.float32)[
        None
    ]
    qkv_sum, mix_sum = (
        lax.psum_scatter(
            qkv_part.astype(jnp.bfloat16), "tp", scatter_dimension=2, tiled=True
        ).astype(jnp.float32),
        lax.psum_scatter(
            mix_part.astype(jnp.bfloat16), "tp", scatter_dimension=2, tiled=True
        ).astype(jnp.float32),
    )
    head_acts = jnp.moveaxis(qkv_sum.astype(jnp.bfloat16), 2, 0)
    grad_mixed = jnp.moveaxis(mix_sum[0].astype(jnp.bfloat16), 1, 0)
    saved_heads = jnp.moveaxis(stored, 2, 0)
    mixed_heads = lax.map(
        lambda pack_in: forward_blocks(pack_in[0][0], pack_in[0][1], pack_in[0][2], pack_in[1]),
        (head_acts, random_rows),
    )
    mixed_part = jnp.moveaxis(mixed_heads, 0, 1)[None]
    head_grads = lax.map(
        lambda pack_in: backward_blocks(
            pack_in[0][0], pack_in[0][1], pack_in[0][2], pack_in[1], pack_in[2]
        ),
        (saved_heads, grad_mixed, random_rows),
    )
    grad_part = jnp.swapaxes(jnp.stack(head_grads, axis=0), 1, 2)
    both_all = lax.all_gather(
        jnp.concatenate([mixed_part, grad_part], axis=0), "tp", axis=2, tiled=True
    )
    front_part = jnp.einsum(
        "lhe,hed->ld", both_all[0], proj_out, preferred_element_type=jnp.float32
    )
    back_part = jnp.einsum(
        "clhe,cdhe->ld", both_all[1:], proj_in, preferred_element_type=jnp.float32
    )
    summed = lax.psum_scatter(
        jnp.stack([front_part, back_part], axis=1).astype(jnp.bfloat16),
        "ctx",
        scatter_dimension=0,
        tiled=True,
    ).astype(jnp.float32)
    fwd_new = (inputs_now.astype(jnp.float32) + summed[:, 0]).astype(jnp.bfloat16)
    fwd_next = pass_on(fwd_new, 1)
    grad_new = (grads_now.astype(jnp.float32) + summed[:, 1]).astype(jnp.bfloat16)
    grad_prev = pass_on(grad_new, -1)
    return (fwd_next[None], grad_prev[None])


def solution(mesh):
    placed = (
        P("section", "ctx", "tp"),
        P("section", "ctx", "tp"),
        P("section", None, "tp", "ctx", None),
        P("section", "ctx", None, "tp"),
        P("section", None, None, ("ctx", "tp"), None),
        P("section", ("ctx", "tp"), None, None),
    )
    return jax.shard_map(
        per_device,
        mesh=mesh,
        in_specs=placed,
        out_specs=(P("section", "ctx", "tp"), P("section", "ctx", "tp")),
        check_vma=False,
    )
```

profile of v0, /device:TPU:65, one launch (start us, length us, event | category | flops | bytes accessed | tf_op | source)
XLA Modules:
  0.0 427.3 jit_solution(13199613929009335173)
XLA Ops:
  8.7 47.5 %all-gather.10.cloned.1.call-done = bf16[1,1024,1536]{2,1,0:T(8,128)(2,1)} async-done(((bf16[1,128,1536]{2,1,0:T(8,128)(2,1)}), bf16[1,1024,1536]{2,1,0:T(8,128)(2,1)}) %all-gather.10.cloned.1.call-update) | async-done | bytes 3145744 | tf_op jit(solution)/shard_map/all_gather | solution.py:156
  56.2 4.7 %fusion.32 = bf16[1,1024,4,128]{3,1,2,0:T(8,128)(2,1)} fusion(bf16[1,4,128,1536]{3,2,1,0:T(8,128)(2,1)S(1)} %copy-done, bf16[1,1024,1536]{2,1,0:T(8,128)(2,1)} %all-gather.10.cloned.1.call-done), kind=kOutput, calls=%fused_computation.38 | convolution fusion | flops 1611137024 | bytes 5767168 | tf_op jit(solution)/shard_map/ld,hed->lhe/dot_general | solution.py:159
  61.0 43.5 %all-gather.8.cloned.1.call-done = bf16[1,1024,1536]{2,1,0:T(8,128)(2,1)} async-done(((bf16[1,128,1536]{2,1,0:T(8,128)(2,1)}), bf16[1,1024,1536]{2,1,0:T(8,128)(2,1)}) %all-gather.8.cloned.1.call-update) | async-done | bytes 3145744 | tf_op jit(solution)/shard_map/all_gather | solution.py:155
  104.5 9.5 %convert_bitcast_fusion = bf16[3,1024,4,128]{1,3,2,0:T(8,128)(2,1)} fusion(bf16[1,1024,1536]{2,1,0:T(8,128)(2,1)} %all-gather.8.cloned.1.call-done, bf16[3,1536,4,128]{3,2,1,0:T(4,128)(2,1)} %bitcast.249), kind=kOutput, calls=%fused_computation.33 | convolution fusion | flops 4833411072 | bytes 11010048 | tf_op jit(solution)/shard_map/ld,cdhe->clhe/dot_general | solution.py:158
  114.9 2.2 gather_fusion.2
  120.5 4.4 %fusion.101 = f32[16,8,64,64]{3,2,1,0:T(8,128)} fusion(bf16[16,8,64,128]{3,2,1,0:T(8,128)(2,1)} %bitcast.229, bf16[16,64,128,1]{2,1,3,0:T(8,128)(2,1)S(1)} %bitcast.234), kind=kOutput, calls=%fused_computation.132 | convolution fusion | flops 134217728 | bytes 4456448 | tf_op jit(solution)/shard_map/while/body/eval_jaxpr/ibe,iake->ibak/dot_general | solution.py:46
  124.9 9.4 %reduce-scatter.6.cloned.1.call-done = bf16[1,1024,1,128]{3,1,2,0:T(8,128)(2,1)} async-done(((bf16[1,1024,4,128]{3,1,2,0:T(8,128)(2,1)}), bf16[1,1024,1,128]{3,1,2,0:T(8,128)(2,1)}) %reduce-scatter.6.cloned.1.call-update) | async-done | bytes 262160 | tf_op jit(solution)/shard_map/reduce_scatter | solution.py:166
  137.3 81.3 %all-reduce.3.cloned.1.call-done = bf16[3,1024,4,128]{1,3,2,0:T(8,128)(2,1)} async-done(((bf16[3,1024,4,128]{1,3,2,0:T(8,128)(2,1)}), bf16[3,1024,4,128]{1,3,2,0:T(8,128)(2,1)}) %all-reduce.3.cloned.1.call-update) | async-done | bytes 3145744
  218.6 2.5 constant_dynamic-slice_fusion
  221.4 2.2 gather_fusion
  223.6 4.3 %fusion.8 = (f32[16,64]{1,0:T(8,128)S(1)}, f32[16,64]{1,0:T(8,128)S(1)}, f32[16,64,8,64]{1,3,2,0:T(8,128)S(1)}) fusion(pred[16,8]{1,0:T(8,128)(4,1)S(1)} %copy.73, f32[16,8,64,64]{3,2,1,0:T(8,128)} %fusion.101, bf16[16,64,128,1]{2,1,3,0:T(8,128)(2,1)S(1)} %bitcast.242, bf16[16,8,64,128]{3,2,1,0:T(8,128)(2,1)} %bitcast.231), kind=kOutput, calls=%fused_computation.23 | convolution fusion | flops 137361408 | bytes 6561920 | tf_op jit(solution)/shard_map/while/body/eval_jaxpr/ibe,iake->ibak/dot_general | solution.py:46
  227.9 2.2 fusion.13
  236.4 2.7 fusion.102
  239.0 2.7 fusion.103
  246.3 4.6 %fusion.37 = bf16[16,64,128]{2,1,0:T(8,128)(2,1)S(1)} fusion(bf16[16,8,64,128]{3,2,1,0:T(8,128)(2,1)} %bitcast.236, f32[16,64,8,64]{1,3,2,0:T(8,128)} %copy-done.5, f32[16,64]{1,0:T(8,128)S(1)} %get-tuple-element.21, f32[16,64]{1,0:T(8,128)S(1)} %get-tuple-element.30, pred[16,8]{1,0:T(8,128)(4,1)S(1)} %copy.73), kind=kOutput, calls=%fused_computation.39 | convolution fusion | flops 136839168 | bytes 4464768 | tf_op jit(solution)/shard_map/while/body/eval_jaxpr/ibak,iake->ibe/dot_general | solution.py:62
  250.9 4.4 %fusion.38 = f32[16,64,128]{2,0,1:T(8,128)S(1)} fusion(f32[16,8,64,128]{3,2,1,0:T(8,128)S(1)} %copy-done.4, s32[16,8]{0,1:T(8,128)S(1)} %pad_add_fusion, pred[16,8]{0,1:T(8,128)(4,1)S(1)} %not.14), kind=kOutput, calls=%fused_computation.40 | convolution fusion | flops 201330688 | bytes 4719232 | tf_op jit(solution)/shard_map/while/body/eval_jaxpr/iaj,iake->jke/dot_general | solution.py:110
  255.8 4.6 %fusion.41 = f32[16,64,128]{2,0,1:T(8,128)S(1)} fusion(f32[16,8,64,128]{3,2,1,0:T(8,128)S(1)} %copy-done.3, s32[16,8]{0,1:T(8,128)S(1)} %pad_add_fusion, pred[16,8]{0,1:T(8,128)(4,1)S(1)} %not.14), kind=kOutput, calls=%fused_computation.41 | convolution fusion | flops 201330688 | bytes 4719232 | tf_op jit(solution)/shard_map/while/body/eval_jaxpr/iaj,iake->jke/dot_general | solution.py:113
  262.6 50.8 %all-gather.6.cloned.1.call-done = bf16[4,1024,4,128]{3,1,0,2:T(8,128)(2,1)} async-done(((bf16[4,1024,1,128]{3,1,0,2:T(8,128)(2,1)}), bf16[4,1024,4,128]{3,1,0,2:T(8,128)(2,1)}) %all-gather.6.cloned.1.call-update) | async-done | bytes 4194320 | tf_op jit(solution)/shard_map/all_gather | solution.py:185
  313.4 3.4 fusion.9
  316.8 7.7 %fusion.10 = bf16[1024,1,1536]{2,0,1:T(8,128)(2,1)S(1)} fusion(bf16[3,1536,4,128]{3,2,1,0:T(4,128)(2,1)} %bitcast.250, bf16[4,1024,4,128]{3,1,0,2:T(8,128)(2,1)S(1)} %copy-done.18), kind=kOutput, calls=%fused_computation.25 | convolution fusion | flops 4833411072 | bytes 11010048 | tf_op jit(solution)/shard_map/clhe,cdhe->ld/dot_general | solution.py:191
  324.6 3.2 pad_maximum_fusion
  327.8 76.0 %reduce-scatter.8.cloned.1.call-done = bf16[128,2,1536]{2,0,1:T(8,128)(2,1)} async-done(((bf16[1024,2,1536]{2,0,1:T(8,128)(2,1)}), bf16[128,2,1536]{2,0,1:T(8,128)(2,1)}) %reduce-scatter.8.cloned.1.call-update) | async-done | bytes 786448 | tf_op jit(solution)/shard_map/reduce_scatter | solution.py:194
  406.1 3.2 collective-permute-start
  409.3 9.7 %collective-permute-done.1 = bf16[128,1536]{1,0:T(8,128)(2,1)S(1)} collective-permute-done((bf16[128,1536]{1,0:T(8,128)(2,1)S(1)}, bf16[128,1536]{1,0:T(8,128)(2,1)S(1)}, u32[]{:S(2)}, u32[]{:S(2)}) %collective-permute-start.1) | collective-permute-done | bytes 393248 | tf_op jit(solution)/shard_map/ppermute | solution.py:15
  (104 shorter events, 26.2 us)
Async XLA Ops:
  7.2 49.1 %copy-start = (bf16[1,4,128,1536]{3,2,1,0:T(8,128)(2,1)S(1)}, bf16[1,4,128,1536]{3,2,1,0:T(8,128)(2,1)}, u32[]{:S(2)}) copy-start(bf16[1,4,128,1536]{3,2,1,0:T(8,128)(2,1)} %param.9) | copy-start | bytes 4718596
  7.2 49.0 %all-gather.10.cloned.1.call-start = ((), (), s32[]{:S(2)}) async-start(), calls=%async_computation.6 | async-start | bytes 3538944 | tf_op jit(solution)/shard_map/all_gather | solution.py:156
  7.9 96.6 %all-gather.8.cloned.1.call-start = ((), (), s32[]{:S(2)}) async-start(), calls=%async_computation.5 | async-start | bytes 3538944 | tf_op jit(solution)/shard_map/all_gather | solution.py:155
  8.7 125.5 %reduce-scatter.6.cloned.1.call-start = ((), (), s32[]{:S(2)}) async-start(), calls=%async_computation.2 | async-start | bytes 1310720 | tf_op jit(solution)/shard_map/reduce_scatter | solution.py:166
  60.9 157.6 %all-reduce.3.cloned.1.call-start = ((), (), s32[]{:S(2)}) async-start(), calls=%async_computation.7 | async-start | bytes 6291456
  104.5 9.8 %copy-start.17 = (s32[1,1,16,3]{2,1,3,0:T(1,128)S(1)}, s32[1,1,16,3]{2,1,3,0:T(1,128)}, u32[]{:S(2)}) copy-start(s32[1,1,16,3]{2,1,3,0:T(1,128)} %param.11) | copy-start | bytes 580
  104.5 10.3 %copy-start.7 = (bf16[1,3,1024,1,128]{4,2,3,1,0:T(8,128)(2,1)S(1)}, bf16[1,3,1024,1,128]{4,2,3,1,0:T(8,128)(2,1)}, u32[]{:S(2)}) copy-start(bf16[1,3,1024,1,128]{4,2,3,1,0:T(8,128)(2,1)} %param.10) | copy-start | bytes 2359300
  114.1 199.3 %all-gather.6.cloned.1.call-start = ((), (), s32[]{:S(2)}) async-start(), calls=%async_computation.3 | async-start | bytes 5242880 | tf_op jit(solution)/shard_map/all_gather | solution.py:185
  114.9 4.3 %copy-start.19 = (u32[256]{0:T(256)S(1)}, u32[256]{0:T(256)}, u32[]{:S(2)}) copy-start(u32[256]{0:T(256)} %constant.88) | copy-start | bytes 3076
  120.2 15.1 %copy-start.8 = (f32[128,1024]{1,0:T(8,128)}, f32[128,1024]{1,0:T(8,128)S(1)}, u32[]{:S(2)}) copy-start(f32[128,1024]{1,0:T(8,128)S(1)} %get-tuple-element.51) | copy-start | bytes 1572868
  223.6 4.4 %copy-start.1 = (f32[16,8,64,64]{3,2,1,0:T(8,128)S(1)}, f32[16,8,64,64]{3,2,1,0:T(8,128)}, u32[]{:S(2)}) copy-start(f32[16,8,64,64]{3,2,1,0:T(8,128)} %fusion.101) | copy-start | bytes 6291460
  239.0 2.7 copy-start.13
  246.3 4.6 %copy-start.4 = (f32[16,8,64,128]{3,2,1,0:T(8,128)S(1)}, f32[16,8,64,128]{3,2,1,0:T(8,128)}, u32[]{:S(2)}) copy-start(f32[16,8,64,128]{3,2,1,0:T(8,128)} %fusion.102) | copy-start | bytes 12582916
  250.9 9.5 %copy-start.16 = (bf16[16,64,128]{2,1,0:T(8,128)(2,1)}, bf16[16,64,128]{2,1,0:T(8,128)(2,1)S(1)}, u32[]{:S(2)}) copy-start(bf16[16,64,128]{2,1,0:T(8,128)(2,1)S(1)} %fusion.37) | copy-start | bytes 786436
  250.9 4.6 %copy-start.15 = (bf16[128,1024]{1,0:T(8,128)(2,1)S(1)}, bf16[128,1024]{1,0:T(8,128)(2,1)}, u32[]{:S(2)}) copy-start(bf16[128,1024]{1,0:T(8,128)(2,1)} %copy-done.14) | copy-start | bytes 786436
  250.9 4.9 %copy-start.3 = (f32[16,8,64,128]{3,2,1,0:T(8,128)S(1)}, f32[16,8,64,128]{3,2,1,0:T(8,128)}, u32[]{:S(2)}) copy-start(f32[16,8,64,128]{3,2,1,0:T(8,128)} %fusion.103) | copy-start | bytes 12582916
  255.3 5.3 %slice-start = ((f32[16,64,128]{2,1,0:T(8,128)}), f32[14,64,128]{2,1,0:T(8,128)S(1)}, s32[]{:S(2)}) async-start(f32[16,64,128]{2,1,0:T(8,128)} %convolution_bitcast_fusion), calls=%async_computation.8 | async-start | bytes 917504 | tf_op jit(solution)/shard_map/while/body/eval_jaxpr/slice | solution.py:130
  255.3 5.4 %copy-start.9 = (f32[128,1024]{1,0:T(8,128)S(1)}, f32[128,1024]{1,0:T(8,128)}, u32[]{:S(2)}) copy-start(f32[128,1024]{1,0:T(8,128)} %copy-done.8) | copy-start | bytes 1572868
  262.6 141.2 %reduce-scatter.8.cloned.1.call-start = ((), (), s32[]{:S(2)}) async-start(), calls=%async_computation.4 | async-start | bytes 7077888 | tf_op jit(solution)/shard_map/reduce_scatter | solution.py:194
  313.4 3.4 copy-start.18
  327.8 77.4 %copy-start.10 = (bf16[1,128,1536]{2,1,0:T(8,128)(2,1)S(1)}, bf16[1,128,1536]{2,1,0:T(8,128)(2,1)}, u32[]{:S(2)}) copy-start(bf16[1,128,1536]{2,1,0:T(8,128)(2,1)} %param.7) | copy-start | bytes 1179652
  327.8 77.4 %copy-start.11 = (bf16[1,128,1536]{2,1,0:T(8,128)(2,1)S(1)}, bf16[1,128,1536]{2,1,0:T(8,128)(2,1)}, u32[]{:S(2)}) copy-start(bf16[1,128,1536]{2,1,0:T(8,128)(2,1)} %param.6) | copy-start | bytes 1179652
  405.4 13.6 %collective-permute-start.1 = (bf16[128,1536]{1,0:T(8,128)(2,1)S(1)}, bf16[128,1536]{1,0:T(8,128)(2,1)S(1)}, u32[]{:S(2)}, u32[]{:S(2)}) collective-permute-start(bf16[128,1536]{1,0:T(8,128)(2,1)S(1)} %get-tuple-element.35), channel_id=1, source_target_pairs={{32,0},{64,32},{96,64},{128,96},{160,128},{192,160},{224,192},{0,2... | collective-permute-start | bytes 1179656 | tf_op jit(solution)/shard_map/ppermute | solution.py:15
  406.1 12.9 %collective-permute-start = (bf16[128,1536]{1,0:T(8,128)(2,1)S(1)}, bf16[128,1536]{1,0:T(8,128)(2,1)S(1)}, u32[]{:S(2)}, u32[]{:S(2)}) collective-permute-start(bf16[128,1536]{1,0:T(8,128)(2,1)S(1)} %get-tuple-element.36), channel_id=1, source_target_pairs={{224,0},{0,32},{32,64},{64,96},{96,128},{128,160},{160,192},{192,2... | collective-permute-start | bytes 1179656 | tf_op jit(solution)/shard_map/ppermute | solution.py:15
  (6 other events, 9.2 us)
Sparse Core Ops, SparseCore 0:
  9.8 46.3 all-gather.9
  58.0 46.4 all-gather.7
  107.1 27.1 reduce-scatter.5
  136.6 81.9 all-reduce.2
  262.7 50.6 all-gather.5
  327.9 75.8 reduce-scatter.7
where the time goes:
time: 431 us; the launch traced here: 427 us
  waiting for transfers between devices  320 us (74%)
  matrix products  62.8 us (15%)
  local copies, waits for them, and re-layouts  15.8 us (4%)
  between operations  14.6 us (3%)
  other arithmetic  10.2 us (2%)
  starting transfers between devices  4.35 us (1%)
    unnamed x7, waiting for transfers between devices  82.7 us
    reduce_scatter x1, waiting for transfers between devices, per_device(): lax.psum_scatter(jnp.stack([front_part, back_part], axis=1).astype(jnp.bf...  76 us
    all_gather x1, waiting for transfers between devices, per_device(): lax.all_gather(jnp.concatenate([mixed_part, grad_part], axis=0), 'tp', ax...  50.8 us
    all_gather x1, waiting for transfers between devices, per_device(): lax.all_gather(grads_now, 'ctx', axis=0, tiled=True)  47.5 us
    all_gather x1, waiting for transfers between devices, per_device(): lax.all_gather(inputs_now, 'ctx', axis=0, tiled=True)  43.5 us
    ppermute x2, waiting for transfers between devices, passed_along(): return lax.ppermute(block, axis, route)  9.67 us
    dot_general x1, matrix products, per_device(): jnp.einsum('ld,cdhe->clhe', all_inputs, proj_in, preferred_element_type=j...  9.53 us
    reduce_scatter x1, waiting for transfers between devices, per_device(): lax.psum_scatter(mix_part.astype(jnp.bfloat16), 'tp', scatter_dimension=2...  9.36 us
  transfers between devices with their start and end apart: 8, of which 7 were waited for; matrix products, arithmetic and copies ran while one was open for 6% of the time, Pallas kernels for 0%

commit v1 on v0

v1 whole, which is shorter than its diff:
```python
import math

import jax
import jax.numpy as jnp
from jax import lax
from jax.experimental import pallas as pl
from jax.experimental.pallas import tpu as pltpu
from jax.sharding import PartitionSpec as P

MESH = pl.DeviceIdType.MESH
F32, BF16 = jnp.float32, jnp.bfloat16
T, TB, W, HD = 1024, 128, 1536, 128
PLACES = ((0, 0), (0, 1), (-1, 0), (1, 0), (-1, 1), (1, 1), (2, 0), (2, 1))
N_SEMS = 144


def nn(a, b):
    return lax.dot_general(a, b, (((1,), (0,)), ((), ())), preferred_element_type=F32)


def nt(a, b):
    return lax.dot_general(a, b, (((1,), (1,)), ((), ())), preferred_element_type=F32)


def tn(a, b):
    return lax.dot_general(a, b, (((0,), (0,)), ((), ())), preferred_element_type=F32)


def kernel(fin, gout, wq, wo_in, sv_in, rnd, fnext, gprev, x_b, x_f, w_raw, wp, wo, sv, bias, probs, head_out,
           yp_b, yp_f, y2u_b, y2u_f, y2d_b, y2d_f, ya_b, ya_f, yb_b, yb_f, act_b, act_f, dk, dv, mixed, grads,
           xs_b, xs_f, rz_b, rz_f, rl_b, rl_f, rr_b, rr_f, out_b, out_f, load_sem, send_sem, recv_sem):
    sec, ctx, tp = lax.axis_index("section"), lax.axis_index("ctx"), lax.axis_index("tp")
    zl, xc = ctx // 4, ctx % 4

    def at_place(dx, dz):
        return (zl + dz) % 2 * 4 + (xc + dx + 4) % 4

    owner = [at_place(*place) for place in PLACES]
    right, left, across = {"ctx": owner[3]}, {"ctx": owner[2]}, {"ctx": owner[1]}
    up, down = {"tp": (tp + 1) % 4}, {"tp": (tp + 3) % 4}
    after, before = {"section": (sec + 1) % 8}, {"section": (sec + 7) % 8}
    scale = 1.0 / math.sqrt(HD)

    loads = []

    def load(src, dst):
        copy = pltpu.make_async_copy(src, dst, load_sem.at[len(loads)])
        loads.append(copy)
        copy.start()
        return copy

    sv_loads = [
        load(sv_in.at[:, pl.ds(pl.multiple_of(owner[s] * TB, TB), TB), :], sv.at[:, pl.ds(s * TB, TB), :])
        for s in range(8)
    ]
    own_loads = [load(gout, x_b.at[pl.ds(0, TB)]), load(fin, x_f.at[pl.ds(0, TB)])]
    wo_loads = [
        load(wo_in.at[pl.ds(pl.multiple_of((tp + j) % 4 * HD, HD), HD), :], wo.at[pl.ds(j * HD, HD), :])
        for j in range(4)
    ]
    wq_load = load(wq, w_raw)

    barrier = pltpu.get_barrier_semaphore()
    for other in (right, left, across, up, down, after, before):
        pl.semaphore_signal(barrier, inc=1, device_id=other, device_id_type=MESH)
    pl.semaphore_wait(barrier, 7)

    sent = []

    def msg(src, dst, other):
        k = len(sent)
        copy = pltpu.make_async_remote_copy(
            src_ref=src, dst_ref=dst, send_sem=send_sem.at[k], recv_sem=recv_sem.at[k],
            device_id=other, device_id_type=MESH,
        )
        sent.append(copy)
        return copy

    def part(ref, s, lo=0, hi=TB):
        return ref.at[pl.ds(s * TB + lo, hi - lo)]

    class Flow:
        pass

    flows = []
    for own, x, yp, y2u, y2d, ya, yb, act, heads, xs, rz, rl, rr, out, dest, hop, w in (
        (gout, x_b, yp_b, y2u_b, y2d_b, ya_b, yb_b, act_b, grads, xs_b, rz_b, rl_b, rr_b, out_b, gprev, before, 128),
        (fin, x_f, yp_f, y2u_f, y2d_f, ya_f, yb_f, act_f, mixed, xs_f, rz_f, rl_f, rr_f, out_f, fnext, after, 384),
    ):
        f = Flow()
        f.x, f.yp, f.y2u, f.y2d, f.ya, f.yb, f.act, f.heads = x, yp, y2u, y2d, ya, yb, act, heads
        f.xs, f.out, f.w = xs, out, w
        f.own_r, f.own_l, f.own_z = msg(own, part(x, 2), right), msg(own, part(x, 3), left), msg(own, part(x, 1), across)
        f.fwd_r = msg(part(x, 2, 0, 96), part(x, 6, 0, 96), right)
        f.fwd_l = msg(part(x, 3, 96, 128), part(x, 6, 96, 128), left)
        f.fwd_z2 = msg(part(x, 2, 64, 128), part(x, 4, 64, 128), across)
        f.fwd_z3 = msg(part(x, 3, 64, 128), part(x, 5, 64, 128), across)
        f.z_r = msg(part(x, 1, 0, 64), part(x, 4, 0, 64), right)
        f.z_l = msg(part(x, 1, 0, 64), part(x, 5, 0, 64), left)
        f.z_l2 = msg(part(x, 5, 0, 64), part(x, 7, 0, 64), left)
        f.far_a = msg(part(x, 6, 64, 96), part(x, 7, 64, 96), across)
        f.far_b = msg(part(x, 6, 96, 128), part(x, 7, 96, 128), across)
        f.s2u, f.s2d, f.s1u, f.s1d, f.hu, f.hd, f.h2u, f.h2d = [], [], [], [], [], [], [], []
        v = 512 - w
        f.v = v
        for g in range(4):
            all_rows = pl.ds(g * 256, 256)
            first, last = pl.ds(g * 256, 128), pl.ds(g * 256 + 128, 128)
            f.s2u.append(msg(yp.at[first, pl.ds(2 * w, w)], y2u.at[pl.ds(g * 128, 128)], up))
            f.s2d.append(msg(yp.at[last, pl.ds(2 * w, w)], y2d.at[pl.ds(g * 128, 128)], down))
            f.s1u.append(msg(yp.at[all_rows, pl.ds(w, w)], ya.at[all_rows], up))
            f.s1d.append(msg(yp.at[all_rows, pl.ds(3 * w, w)], yb.at[all_rows], down))
            f.hu.append(msg(heads.at[all_rows, pl.ds(0, v)], heads.at[all_rows, pl.ds(3 * v, v)], up))
            f.hd.append(msg(heads.at[all_rows, pl.ds(0, v)], heads.at[all_rows, pl.ds(v, v)], down))
            f.h2u.append(msg(heads.at[first, pl.ds(3 * v, v)], heads.at[first, pl.ds(2 * v, v)], up))
            f.h2d.append(msg(heads.at[last, pl.ds(v, v)], heads.at[last, pl.ds(2 * v, v)], down))
        f.zb6, f.zb2, f.zb3, f.z0 = (rz.at[pl.ds(a, n)] for a, n in ((0, 64), (64, 64), (128, 64), (192, 128)))
        f.la5, f.la1, f.l3, f.l0 = (rl.at[pl.ds(a, n)] for a, n in ((0, 64), (64, 64), (128, 32), (160, 128)))
        f.ra1, f.r2, f.r0 = (rr.at[pl.ds(a, n)] for a, n in ((0, 64), (64, 96), (160, 128)))
        f.t7r, f.t7z = msg(part(xs, 7, 0, 64), f.la5, right), msg(part(xs, 7, 64, 128), f.zb6, across)
        f.t6l, f.t6r = msg(part(xs, 6, 0, 96), f.r2, left), msg(part(xs, 6, 96, 128), f.l3, right)
        f.t5r, f.t5z = msg(part(xs, 5, 0, 64), f.la1, right), msg(part(xs, 5, 64, 128), f.zb3, across)
        f.t4l, f.t4z = msg(part(xs, 4, 0, 64), f.ra1, left), msg(part(xs, 4, 64, 128), f.zb2, across)
        f.t3r, f.t2l, f.t1z = msg(part(xs, 3), f.l0, right), msg(part(xs, 2), f.r0, left), msg(part(xs, 1), f.z0, across)
        f.hop = msg(out, dest, hop)
        flows.append(f)
    fb, ff = flows

    def start(*copies):
        for copy in copies:
            copy.start()

    def got(*copies):
        for copy in copies:
            copy.wait_recv()

    def send_own(f):
        start(f.own_r, f.own_l, f.own_z)

    def forward_near(f):
        got(f.own_r, f.own_l, f.own_z)
        start(f.fwd_r, f.z_l, f.fwd_z2, f.z_r, f.fwd_z3, f.fwd_l)

    def forward_far(f):
        got(f.z_l)
        start(f.z_l2)
        got(f.fwd_l)
        start(f.far_b)
        got(f.fwd_r)
        start(f.far_a)

    def add_into(dst, lo, n, srcs, cols=None):
        @pl.loop(0, n // 16)
        def _(i):
            r = pl.ds(lo + pl.multiple_of(i * 16, 16), 16)
            c = slice(None) if cols is None else cols
            total = dst[r, c].astype(F32)
            for src in srcs:
                total = total + src[pl.ds(pl.multiple_of(i * 16, 16), 16), :].astype(F32)
            dst[r, c] = total.astype(BF16)

    def project(f, g):
        r = pl.ds(g * 256, 256)

        @pl.loop(0, 4 * f.w // 256)
        def _(n):
            c = pl.ds(pl.multiple_of(n * 256, 256), 256)
            p = nn(f.x[r, :], wp[:, c]) if f is ff else nt(f.x[r, :], wo[c, :])
            f.yp[r, c] = p.astype(BF16)

        start(f.s2u[g], f.s2d[g])

    def sum_two(f, g):
        got(f.s2u[g])
        add_into(f.yp, g * 256, 128, [f.y2u.at[pl.ds(g * 128, 128)]], pl.ds(f.w, f.w))
        start(f.s1u[g])
        got(f.s2d[g])
        add_into(f.yp, g * 256 + 128, 128, [f.y2d.at[pl.ds(g * 128, 128)]], pl.ds(3 * f.w, f.w))
        start(f.s1d[g])

    def sum_all(f, g):
        got(f.s1u[g], f.s1d[g])

        @pl.loop(0, 16)
        def _(i):
            r = pl.ds(g * 256 + pl.multiple_of(i * 16, 16), 16)
            total = f.yp[r, pl.ds(0, f.w)].astype(F32) + f.ya[r, :].astype(F32) + f.yb[r, :].astype(F32)
            f.act[r, :] = total.astype(BF16)

    def make_bias():
        lane = lax.broadcasted_iota(jnp.int32, (8, T), 1)
        key = lane // 64 % 2
        for s in range(8):
            key = key + jnp.where(lane // TB == s, 2 * owner[s], 0)
        for s in range(8):
            for half in range(2):
                q = 2 * owner[s] + half
                ok = (key < 2) | (key == q) | (key == (q + 1) % 16) | (key == (q + 15) % 16)
                for n in range(3):
                    ok = ok | (key == rnd[q, n])
                ok = ok | (jnp.full((8, T), q, jnp.int32) < 2)
                bias[2 * s + half] = jnp.where(ok, 0.0, -1e30).astype(F32)

    def softmax(q, k, b0):
        n = q.shape[0] // 64
        s = nt(q, k).reshape(n, 8, 8, T) * scale + bias[pl.ds(b0, n)].reshape(n, 1, 8, T)
        s = s.reshape(n * 64, T)
        e = jnp.exp(s - jnp.max(s, axis=-1, keepdims=True))
        return (e * (1.0 / jnp.sum(e, axis=-1, keepdims=True))).astype(BF16)

    def saved_probs():
        @pl.loop(0, 8)
        def _(i):
            r = pl.ds(pl.multiple_of(i * 128, 128), 128)
            p = softmax(sv[0, r, :], sv[1], i * 2)
            probs[r, :] = p
            head_out[r, :] = nn(p, sv[2]).astype(BF16)

    def backward_head():
        dk[...] = jnp.zeros_like(dk)
        dv[...] = jnp.zeros_like(dv)

        @pl.loop(0, 4)
        def _(i):
            r = pl.ds(pl.multiple_of(i * 256, 256), 256)
            g = act_b[r, :]
            delta = jnp.sum(g.astype(F32) * head_out[r, :].astype(F32), axis=-1, keepdims=True)
            p = probs[r, :]
            ds = (p.astype(F32) * (nt(g, sv[2]) - delta)).astype(BF16)
            grads[r, pl.ds(0, HD)] = (nn(ds, sv[1]) * scale).astype(BF16)
            dk[...] += tn(ds, sv[0, r, :])
            dv[...] += tn(p, g)

        grads[:, pl.ds(HD, HD)] = (dk[...] * scale).astype(BF16)
        grads[:, pl.ds(2 * HD, HD)] = dv[...].astype(BF16)

    def forward_head(g):
        @pl.loop(0, 2)
        def _(i):
            r = pl.ds(g * 256 + pl.multiple_of(i * 128, 128), 128)
            p = softmax(act_f[r, pl.ds(0, HD)], act_f[:, pl.ds(HD, HD)], g * 4 + i * 2)
            mixed[r, pl.ds(0, HD)] = nn(p, act_f[:, pl.ds(2 * HD, HD)]).astype(BF16)

    def heads_out(f, g):
        start(f.hu[g], f.hd[g])

    def heads_on(f, g):
        got(f.hu[g])
        start(f.h2u[g])
        got(f.hd[g])
        start(f.h2d[g])

    def order_weights():
        row, col = lax.broadcasted_iota(jnp.int32, (256, 256), 0), lax.broadcasted_iota(jnp.int32, (256, 256), 1)
        pick = jnp.where(col == row % 64 * 4 + (row // 64 + tp) % 4, 1.0, 0.0).astype(BF16)
        for c in range(3):
            @pl.loop(0, 12)
            def _(i):
                a = w_raw[pl.ds(pl.multiple_of((c * 24 + i * 2) * 256, 256), 256), :]
                b = w_raw[pl.ds(pl.multiple_of((c * 24 + i * 2 + 1) * 256, 256), 256), :]
                o = nn(pick, jnp.concatenate([a, b], axis=1)).astype(BF16)
                for j in range(4):
                    for k in range(2):
                        wp[pl.ds(pl.multiple_of(i * 128, 128) + k * 64, 64), pl.ds(j * 384 + c * HD, HD)] = (
                            o[j * 64:j * 64 + 64, k * HD:k * HD + HD]
                        )

    def project_back(f, g):
        got(f.h2u[g], f.h2d[g])
        r = pl.ds(g * 256, 256)

        @pl.loop(0, 6)
        def _(n):
            c = pl.ds(pl.multiple_of(n * 256, 256), 256)
            p = nn(f.heads[r, :], wo[:, c]) if f is ff else nt(f.heads[r, :], wp[c, :])
            f.xs[r, c] = p.astype(BF16)

    def back_3(f):
        project_back(f, 3)
        start(f.t7z, f.t7r)

    def back_2(f):
        project_back(f, 2)
        start(f.t4l, f.t5z, f.t4z)
        got(f.t7z)
        add_into(f.xs, 6 * TB + 64, 64, [f.zb6])
        start(f.t6l, f.t6r)
        got(f.t7r)
        add_into(f.xs, 5 * TB, 64, [f.la5])
        start(f.t5r)

    def back_1(f):
        project_back(f, 1)
        got(f.t5z, f.t6r)
        add_into(f.xs, 3 * TB + 64, 64, [f.zb3])
        add_into(f.xs, 3 * TB + 96, 32, [f.l3])
        start(f.t3r)
        got(f.t4z, f.t6l)
        add_into(f.xs, 2 * TB + 64, 64, [f.zb2])
        add_into(f.xs, 2 * TB, 96, [f.r2])
        start(f.t2l)

    def back_0(f):
        project_back(f, 0)
        got(f.t5r, f.t4l)
        add_into(f.xs, TB, 64, [f.la1, f.ra1])
        start(f.t1z)

    def finish(f):
        got(f.t3r, f.t2l, f.t1z)

        @pl.loop(0, 8)
        def _(i):
            r = pl.ds(pl.multiple_of(i * 16, 16), 16)
            total = f.xs[r, :].astype(F32) + f.x[r, :].astype(F32)
            for src in (f.l0, f.r0, f.z0):
                total = total + src[r, :].astype(F32)
            f.out[r, :] = total.astype(BF16)

        start(f.hop)

    send_own(fb)
    make_bias()
    for copy in sv_loads:
        copy.wait()
    saved_probs()
    for copy in own_loads + wo_loads:
        copy.wait()
    forward_near(fb)
    project(fb, 0)
    forward_far(fb)
    send_own(ff)
    project(fb, 1)
    sum_two(fb, 0)
    wq_load.wait()
    order_weights()
    got(fb.z_r, fb.fwd_z2, fb.fwd_z3)
    project(fb, 2)
    sum_two(fb, 1)
    sum_all(fb, 0)
    got(fb.z_l2, fb.far_a, fb.far_b)
    project(fb, 3)
    sum_two(fb, 2)
    sum_all(fb, 1)
    forward_near(ff)
    sum_two(fb, 3)
    sum_all(fb, 2)
    project(ff, 0)
    sum_all(fb, 3)
    backward_head()
    for g in (3, 2, 1, 0):
        heads_out(fb, g)
    forward_far(ff)
    project(ff, 1)
    sum_two(ff, 0)
    heads_on(fb, 3)
    got(ff.z_r, ff.fwd_z2, ff.fwd_z3)
    project(ff, 2)
    sum_two(ff, 1)
    heads_on(fb, 2)
    got(ff.z_l2, ff.far_a, ff.far_b)
    project(ff, 3)
    sum_two(ff, 2)
    sum_all(ff, 0)
    heads_on(fb, 1)
    back_3(fb)
    sum_two(ff, 3)
    sum_all(ff, 1)
    heads_on(fb, 0)
    back_2(fb)
    sum_all(ff, 2)
    sum_all(ff, 3)
    for g in (3, 2, 1, 0):
        forward_head(g)
        heads_out(ff, g)
    back_1(fb)
    heads_on(ff, 3)
    heads_on(ff, 2)
    back_0(fb)
    heads_on(ff, 1)
    heads_on(ff, 0)
    back_3(ff)
    back_2(ff)
    finish(fb)
    back_1(ff)
    back_0(ff)
    finish(ff)
    got(fb.hop, ff.hop)
    for copy in sent:
        copy.wait_send()
    assert len(sent) <= N_SEMS


def per_device(fwd_input, grad_out, w_qkv, w_out, saved_qkv, rand_blocks):
    def vmem(*shape, dtype=BF16):
        return pltpu.VMEM(shape, dtype)

    def pair(rows, width_b, width_f):
        return [vmem(rows, width_b), vmem(rows, width_f)]

    any_space = pl.BlockSpec(memory_space=pl.ANY)
    fwd_next, grad_prev = pl.pallas_call(
        kernel,
        out_shape=[jax.ShapeDtypeStruct((TB, W), BF16)] * 2,
        in_specs=[any_space] * 5 + [pl.BlockSpec(memory_space=pltpu.SMEM)],
        out_specs=[any_space] * 2,
        scratch_shapes=[
            *pair(T, W, W), vmem(12 * W, HD), vmem(W, W), vmem(512, W), vmem(3, T, HD),
            vmem(16, 8, T, dtype=F32), vmem(T, T), vmem(T, HD),
            *pair(T, 512, 1536), *pair(512, 128, 384), *pair(512, 128, 384), *pair(T, 128, 384), *pair(T, 128, 384),
            *pair(T, 128, 384), vmem(T, HD, dtype=F32), vmem(T, HD, dtype=F32), vmem(T, 512), vmem(T, 1536),
            *pair(T, W, W), *pair(320, W, W), *pair(288, W, W), *pair(288, W, W), *pair(TB, W, W),
            pltpu.SemaphoreType.DMA((16,)), pltpu.SemaphoreType.DMA((N_SEMS,)), pltpu.SemaphoreType.DMA((N_SEMS,)),
        ],
        compiler_params=pltpu.CompilerParams(
            collective_id=0, has_side_effects=True, vmem_limit_bytes=62 * 1024 * 1024
        ),
        cost_estimate=pl.CostEstimate(flops=16_000_000_000, bytes_accessed=10_000_000, transcendentals=2_000_000),
    )(
        fwd_input.reshape(TB, W),
        grad_out.reshape(TB, W),
        w_qkv.reshape(12 * W, HD),
        w_out.reshape(512, W),
        saved_qkv.reshape(3, T, HD),
        rand_blocks.reshape(16, 3),
    )
    return (fwd_next[None], grad_prev[None])


def solution(mesh):
    placed = (
        P("section", "ctx", "tp"),
        P("section", "ctx", "tp"),
        P("section", None, "tp", "ctx", None),
        P("section", "ctx", None, "tp"),
        P("section", None, None, ("ctx", "tp"), None),
        P("section", ("ctx", "tp"), None, None),
    )
    return jax.shard_map(
        per_device,
        mesh=mesh,
        in_specs=placed,
        out_specs=(P("section", "ctx", "tp"), P("section", "ctx", "tp")),
        check_vma=False,
    )
```

time: 431 us -> 160 us (0.37)
  the two profiles are of different devices: /device:TPU:65 before, /device:TPU:161 now
where the time goes in v1:
time: 160 us
  Pallas kernels  154 us (96%)
  local copies, waits for them, and re-layouts  4.89 us (3%)
    pallas_call x1, Pallas kernels, per_device(): pl.pallas_call(kernel, out_shape=[jax.ShapeDtypeStruct((TB, W), BF16)] *...  154 us
    unnamed x2, local copies, waits for them, and re-layouts  3.53 us

profile of v1, /device:TPU:161, one launch (start us, length us, event | category | flops | bytes accessed | tf_op | source)
XLA Modules:
  0.0 159.9 jit_solution(14302398571254797388)
XLA Ops:
  0.6 1.4 copy.9
  2.0 154.3 %shard_map.77 = (bf16[128,1536]{1,0:T(8,128)(2,1)}, bf16[128,1536]{1,0:T(8,128)(2,1)}) custom-call(bf16[128,1536]{1,0:T(8,128)(2,1)} %bitcast.14, bf16[128,1536]{1,0:T(8,128)(2,1)} %bitcast.15, bf16[18432,128]{1,0:T(8,128)(2,1)} %bitcast.11, bf16[512,1536]{1,0:T(8,128)(2,1)} %bitcast.12, bf16[3,1024,128]{2,1,0:T(8,128)(2,1)} %bitcast.13, s32[16,3]{1,0:T(8,128)} %bitcast.10), custom_call_target="tpu_custom_call" | custom-call | flops 16000000000 | bytes 10000000 | tf_op jit(solution)/shard_map/pallas_call | solution.py:402
  156.3 1.8 %copy.12 = bf16[1,128,1536]{2,1,0:T(8,128)(2,1)} copy(bf16[1,128,1536]{2,1,0:T(8,128)(2,1)} %bitcast.9) | data formatting | bytes 786432
  158.1 1.8 %copy.13 = bf16[1,128,1536]{2,1,0:T(8,128)(2,1)} copy(bf16[1,128,1536]{2,1,0:T(8,128)(2,1)} %bitcast.8) | data formatting | bytes 786432

commit v2 on v1

--- a/solution.py
+++ b/solution.py
@@ -11,7 +11,10 @@
 F32, BF16 = jnp.float32, jnp.bfloat16
 T, TB, W, HD = 1024, 128, 1536, 128
 PLACES = ((0, 0), (0, 1), (-1, 0), (1, 0), (-1, 1), (1, 1), (2, 0), (2, 1))
-N_SEMS = 144
+GROUPS = ((0, 1), (1, 1), (2, 2), (4, 2), (6, 2))
+CUT, MID = 64, 96
+LOW = TB - CUT
+N_SEMS = 160
 
 
 def nn(a, b):
@@ -38,7 +41,8 @@
     owner = [at_place(*place) for place in PLACES]
     right, left, across = {"ctx": owner[3]}, {"ctx": owner[2]}, {"ctx": owner[1]}
     up, down = {"tp": (tp + 1) % 4}, {"tp": (tp + 3) % 4}
-    after, before = {"section": (sec + 1) % 8}, {"section": (sec + 7) % 8}
+    sections = lax.axis_size("section")
+    after, before = {"section": (sec + 1) % sections}, {"section": (sec + sections - 1) % sections}
     scale = 1.0 / math.sqrt(HD)
 
     loads = []
@@ -90,39 +94,52 @@
         f = Flow()
         f.x, f.yp, f.y2u, f.y2d, f.ya, f.yb, f.act, f.heads = x, yp, y2u, y2d, ya, yb, act, heads
         f.xs, f.out, f.w = xs, out, w
-        f.own_r, f.own_l, f.own_z = msg(own, part(x, 2), right), msg(own, part(x, 3), left), msg(own, part(x, 1), across)
-        f.fwd_r = msg(part(x, 2, 0, 96), part(x, 6, 0, 96), right)
-        f.fwd_l = msg(part(x, 3, 96, 128), part(x, 6, 96, 128), left)
-        f.fwd_z2 = msg(part(x, 2, 64, 128), part(x, 4, 64, 128), across)
-        f.fwd_z3 = msg(part(x, 3, 64, 128), part(x, 5, 64, 128), across)
-        f.z_r = msg(part(x, 1, 0, 64), part(x, 4, 0, 64), right)
-        f.z_l = msg(part(x, 1, 0, 64), part(x, 5, 0, 64), left)
-        f.z_l2 = msg(part(x, 5, 0, 64), part(x, 7, 0, 64), left)
-        f.far_a = msg(part(x, 6, 64, 96), part(x, 7, 64, 96), across)
-        f.far_b = msg(part(x, 6, 96, 128), part(x, 7, 96, 128), across)
+        own_part = {0: own.at[pl.ds(0, CUT)], CUT: own.at[pl.ds(CUT, LOW)]}
+
+        def both(s, other):
+            return [msg(own_part[lo], part(x, s, lo, hi), other) for lo, hi in ((0, CUT), (CUT, TB))]
+
+        f.own_r, f.own_l, f.own_z = both(2, right), both(3, left), both(1, across)
+        f.fwd_r = msg(part(x, 2, 0, CUT), part(x, 6, 0, CUT), right)
+        f.fwd_rq = msg(part(x, 2, CUT, MID), part(x, 6, CUT, MID), right)
+        f.fwd_l = msg(part(x, 3, MID, TB), part(x, 6, MID, TB), left)
+        f.fwd_z2 = msg(part(x, 2, CUT, TB), part(x, 4, CUT, TB), across)
+        f.fwd_z3 = msg(part(x, 3, CUT, TB), part(x, 5, CUT, TB), across)
+        f.z_r = msg(part(x, 1, 0, CUT), part(x, 4, 0, CUT), right)
+        f.z_l = msg(part(x, 1, 0, CUT), part(x, 5, 0, CUT), left)
+        f.z_l2 = msg(part(x, 5, 0, CUT), part(x, 7, 0, CUT), left)
+        f.far_a = msg(part(x, 6, CUT, MID), part(x, 7, CUT, MID), across)
+        f.far_b = msg(part(x, 6, MID, TB), part(x, 7, MID, TB), across)
         f.s2u, f.s2d, f.s1u, f.s1d, f.hu, f.hd, f.h2u, f.h2d = [], [], [], [], [], [], [], []
         v = 512 - w
         f.v = v
-        for g in range(4):
-            all_rows = pl.ds(g * 256, 256)
-            first, last = pl.ds(g * 256, 128), pl.ds(g * 256 + 128, 128)
-            f.s2u.append(msg(yp.at[first, pl.ds(2 * w, w)], y2u.at[pl.ds(g * 128, 128)], up))
-            f.s2d.append(msg(yp.at[last, pl.ds(2 * w, w)], y2d.at[pl.ds(g * 128, 128)], down))
+        for at, n in GROUPS:
+            all_rows, half = pl.ds(at * TB, n * TB), pl.ds(at * TB // 2, n * TB // 2)
+            first, last = pl.ds(at * TB, n * TB // 2), pl.ds(at * TB + n * TB // 2, n * TB // 2)
+            f.s2u.append(msg(yp.at[first, pl.ds(2 * w, w)], y2u.at[half], up))
+            f.s2d.append(msg(yp.at[last, pl.ds(2 * w, w)], y2d.at[half], down))
             f.s1u.append(msg(yp.at[all_rows, pl.ds(w, w)], ya.at[all_rows], up))
             f.s1d.append(msg(yp.at[all_rows, pl.ds(3 * w, w)], yb.at[all_rows], down))
             f.hu.append(msg(heads.at[all_rows, pl.ds(0, v)], heads.at[all_rows, pl.ds(3 * v, v)], up))
             f.hd.append(msg(heads.at[all_rows, pl.ds(0, v)], heads.at[all_rows, pl.ds(v, v)], down))
             f.h2u.append(msg(heads.at[first, pl.ds(3 * v, v)], heads.at[first, pl.ds(2 * v, v)], up))
             f.h2d.append(msg(heads.at[last, pl.ds(v, v)], heads.at[last, pl.ds(2 * v, v)], down))
-        f.zb6, f.zb2, f.zb3, f.z0 = (rz.at[pl.ds(a, n)] for a, n in ((0, 64), (64, 64), (128, 64), (192, 128)))
-        f.la5, f.la1, f.l3, f.l0 = (rl.at[pl.ds(a, n)] for a, n in ((0, 64), (64, 64), (128, 32), (160, 128)))
-        f.ra1, f.r2, f.r0 = (rr.at[pl.ds(a, n)] for a, n in ((0, 64), (64, 96), (160, 128)))
-        f.t7r, f.t7z = msg(part(xs, 7, 0, 64), f.la5, right), msg(part(xs, 7, 64, 128), f.zb6, across)
-        f.t6l, f.t6r = msg(part(xs, 6, 0, 96), f.r2, left), msg(part(xs, 6, 96, 128), f.l3, right)
-        f.t5r, f.t5z = msg(part(xs, 5, 0, 64), f.la1, right), msg(part(xs, 5, 64, 128), f.zb3, across)
-        f.t4l, f.t4z = msg(part(xs, 4, 0, 64), f.ra1, left), msg(part(xs, 4, 64, 128), f.zb2, across)
-        f.t3r, f.t2l, f.t1z = msg(part(xs, 3), f.l0, right), msg(part(xs, 2), f.r0, left), msg(part(xs, 1), f.z0, across)
-        f.hop = msg(out, dest, hop)
+        def cuts(ref, *sizes):
+            at = [sum(sizes[:i]) for i in range(len(sizes))]
+            return [ref.at[pl.ds(lo, n)] for lo, n in zip(at, sizes)]
+
+        f.zb6, f.zb2, f.zb3, f.z0a, f.z0b = cuts(rz, LOW, LOW, LOW, CUT, LOW)
+        f.la5, f.la1, f.l3, f.l0a, f.l0b = cuts(rl, CUT, CUT, TB - MID, CUT, LOW)
+        f.ra1, f.r2a, f.r2q, f.r0a, f.r0b = cuts(rr, CUT, CUT, MID - CUT, CUT, LOW)
+        f.t7r, f.t7z = msg(part(xs, 7, 0, CUT), f.la5, right), msg(part(xs, 7, CUT, TB), f.zb6, across)
+        f.t6l, f.t6q = msg(part(xs, 6, 0, CUT), f.r2a, left), msg(part(xs, 6, CUT, MID), f.r2q, left)
+        f.t6r = msg(part(xs, 6, MID, TB), f.l3, right)
+        f.t5r, f.t5z = msg(part(xs, 5, 0, CUT), f.la1, right), msg(part(xs, 5, CUT, TB), f.zb3, across)
+        f.t4l, f.t4z = msg(part(xs, 4, 0, CUT), f.ra1, left), msg(part(xs, 4, CUT, TB), f.zb2, across)
+        f.t3a, f.t3b = msg(part(xs, 3, 0, CUT), f.l0a, right), msg(part(xs, 3, CUT, TB), f.l0b, right)
+        f.t2a, f.t2b = msg(part(xs, 2, 0, CUT), f.r0a, left), msg(part(xs, 2, CUT, TB), f.r0b, left)
+        f.t1a, f.t1b = msg(part(xs, 1, 0, CUT), f.z0a, across), msg(part(xs, 1, CUT, TB), f.z0b, across)
+        f.hops = [msg(out.at[r], dest.at[r], hop) for r in (pl.ds(0, CUT), pl.ds(CUT, LOW))]
         flows.append(f)
     fb, ff = flows
 
@@ -135,19 +152,36 @@
             copy.wait_recv()
 
     def send_own(f):
-        start(f.own_r, f.own_l, f.own_z)
-
-    def forward_near(f):
-        got(f.own_r, f.own_l, f.own_z)
-        start(f.fwd_r, f.z_l, f.fwd_z2, f.z_r, f.fwd_z3, f.fwd_l)
-
-    def forward_far(f):
+        start(f.own_z[0], f.own_r[1], f.own_l[1], f.own_z[1], f.own_r[0], f.own_l[0])
+
+    def pass_low(f):
+        got(f.own_r[1], f.own_l[1])
+        start(f.fwd_z2, f.fwd_z3, f.fwd_rq, f.fwd_l)
+        got(f.own_z[0])
+        start(f.z_l, f.z_r)
+
+    def pass_high(f):
+        got(f.own_r[0])
+        start(f.fwd_r)
+
+    def pass_far_low(f):
+        got(f.fwd_l)
+        start(f.far_b)
+        got(f.fwd_rq)
+        start(f.far_a)
+
+    def pass_far_high(f):
         got(f.z_l)
         start(f.z_l2)
-        got(f.fwd_l)
-        start(f.far_b)
-        got(f.fwd_r)
-        start(f.far_a)
+
+    def near_here(f):
+        got(f.own_z[1], f.own_l[0])
+
+    def diagonal_here(f):
+        got(f.z_r, f.fwd_z2, f.fwd_z3)
+
+    def far_here(f):
+        got(f.fwd_r, f.z_l2, f.far_a, f.far_b)
 
     def add_into(dst, lo, n, srcs, cols=None):
         @pl.loop(0, n // 16)
@@ -159,8 +193,11 @@
                 total = total + src[pl.ds(pl.multiple_of(i * 16, 16), 16), :].astype(F32)
             dst[r, c] = total.astype(BF16)
 
+    def rows_of(g):
+        return pl.ds(GROUPS[g][0] * TB, GROUPS[g][1] * TB)
+
     def project(f, g):
-        r = pl.ds(g * 256, 256)
+        r = rows_of(g)
 
         @pl.loop(0, 4 * f.w // 256)
         def _(n):
@@ -171,19 +208,20 @@
         start(f.s2u[g], f.s2d[g])
 
     def sum_two(f, g):
+        at, n = GROUPS[g][0] * TB, GROUPS[g][1] * TB // 2
         got(f.s2u[g])
-        add_into(f.yp, g * 256, 128, [f.y2u.at[pl.ds(g * 128, 128)]], pl.ds(f.w, f.w))
+        add_into(f.yp, at, n, [f.y2u.at[pl.ds(at // 2, n)]], pl.ds(f.w, f.w))
         start(f.s1u[g])
         got(f.s2d[g])
-        add_into(f.yp, g * 256 + 128, 128, [f.y2d.at[pl.ds(g * 128, 128)]], pl.ds(3 * f.w, f.w))
+        add_into(f.yp, at + n, n, [f.y2d.at[pl.ds(at // 2, n)]], pl.ds(3 * f.w, f.w))
         start(f.s1d[g])
 
     def sum_all(f, g):
         got(f.s1u[g], f.s1d[g])
 
-        @pl.loop(0, 16)
+        @pl.loop(0, GROUPS[g][1] * 8)
         def _(i):
-            r = pl.ds(g * 256 + pl.multiple_of(i * 16, 16), 16)
+            r = pl.ds(GROUPS[g][0] * TB + pl.multiple_of(i * 16, 16), 16)
             total = f.yp[r, pl.ds(0, f.w)].astype(F32) + f.ya[r, :].astype(F32) + f.yb[r, :].astype(F32)
             f.act[r, :] = total.astype(BF16)
 
@@ -197,7 +235,7 @@
                 q = 2 * owner[s] + half
                 ok = (key < 2) | (key == q) | (key == (q + 1) % 16) | (key == (q + 15) % 16)
                 for n in range(3):
-                    ok = ok | (key == rnd[q, n])
+                    ok = ok | (key == rnd[n, 0, q])
                 ok = ok | (jnp.full((8, T), q, jnp.int32) < 2)
                 bias[2 * s + half] = jnp.where(ok, 0.0, -1e30).astype(F32)
 
@@ -208,8 +246,8 @@
         e = jnp.exp(s - jnp.max(s, axis=-1, keepdims=True))
         return (e * (1.0 / jnp.sum(e, axis=-1, keepdims=True))).astype(BF16)
 
-    def saved_probs():
-        @pl.loop(0, 8)
+    def saved_probs(quarter):
+        @pl.loop(quarter * 2, quarter * 2 + 2)
         def _(i):
             r = pl.ds(pl.multiple_of(i * 128, 128), 128)
             p = softmax(sv[0, r, :], sv[1], i * 2)
@@ -235,10 +273,10 @@
         grads[:, pl.ds(2 * HD, HD)] = dv[...].astype(BF16)
 
     def forward_head(g):
-        @pl.loop(0, 2)
+        @pl.loop(0, GROUPS[g][1])
         def _(i):
-            r = pl.ds(g * 256 + pl.multiple_of(i * 128, 128), 128)
-            p = softmax(act_f[r, pl.ds(0, HD)], act_f[:, pl.ds(HD, HD)], g * 4 + i * 2)
+            r = pl.ds(GROUPS[g][0] * TB + pl.multiple_of(i * TB, TB), TB)
+            p = softmax(act_f[r, pl.ds(0, HD)], act_f[:, pl.ds(HD, HD)], (GROUPS[g][0] + i) * 2)
             mixed[r, pl.ds(0, HD)] = nn(p, act_f[:, pl.ds(2 * HD, HD)]).astype(BF16)
 
     def heads_out(f, g):
@@ -254,7 +292,7 @@
         row, col = lax.broadcasted_iota(jnp.int32, (256, 256), 0), lax.broadcasted_iota(jnp.int32, (256, 256), 1)
         pick = jnp.where(col == row % 64 * 4 + (row // 64 + tp) % 4, 1.0, 0.0).astype(BF16)
         for c in range(3):
-            @pl.loop(0, 12)
+            @pl.loop(0, 12, unroll=4)
             def _(i):
                 a = w_raw[pl.ds(pl.multiple_of((c * 24 + i * 2) * 256, 256), 256), :]
                 b = w_raw[pl.ds(pl.multiple_of((c * 24 + i * 2 + 1) * 256, 256), 256), :]
@@ -267,7 +305,7 @@
 
     def project_back(f, g):
         got(f.h2u[g], f.h2d[g])
-        r = pl.ds(g * 256, 256)
+        r = rows_of(g)
 
         @pl.loop(0, 6)
         def _(n):
@@ -275,120 +313,188 @@
             p = nn(f.heads[r, :], wo[:, c]) if f is ff else nt(f.heads[r, :], wp[c, :])
             f.xs[r, c] = p.astype(BF16)
 
+    def back_4(f):
+        project_back(f, 4)
+        start(f.t7z, f.t7r, f.t6l)
+
+    def add_4z(f):
+        got(f.t7z)
+        add_into(f.xs, 6 * TB + CUT, LOW, [f.zb6])
+        start(f.t6q, f.t6r)
+
     def back_3(f):
         project_back(f, 3)
-        start(f.t7z, f.t7r)
+        start(f.t5z, f.t4z, f.t4l)
+
+    def add_3x(f):
+        got(f.t7r)
+        add_into(f.xs, 5 * TB, CUT, [f.la5])
+        start(f.t5r)
 
     def back_2(f):
         project_back(f, 2)
-        start(f.t4l, f.t5z, f.t4z)
-        got(f.t7z)
-        add_into(f.xs, 6 * TB + 64, 64, [f.zb6])
-        start(f.t6l, f.t6r)
-        got(f.t7r)
-        add_into(f.xs, 5 * TB, 64, [f.la5])
-        start(f.t5r)
+        start(f.t3a)
+
+    def add_2x(f):
+        got(f.t6l)
+        add_into(f.xs, 2 * TB, CUT, [f.r2a])
+        start(f.t2a)
+
+    def add_2z(f):
+        got(f.t5z, f.t6r)
+        add_into(f.xs, 3 * TB + CUT, LOW, [f.zb3])
+        add_into(f.xs, 3 * TB + MID, TB - MID, [f.l3])
+        start(f.t3b)
+        got(f.t4z, f.t6q)
+        add_into(f.xs, 2 * TB + CUT, LOW, [f.zb2])
+        add_into(f.xs, 2 * TB + CUT, MID - CUT, [f.r2q])
+        start(f.t2b)
 
     def back_1(f):
         project_back(f, 1)
-        got(f.t5z, f.t6r)
-        add_into(f.xs, 3 * TB + 64, 64, [f.zb3])
-        add_into(f.xs, 3 * TB + 96, 32, [f.l3])
-        start(f.t3r)
-        got(f.t4z, f.t6l)
-        add_into(f.xs, 2 * TB + 64, 64, [f.zb2])
-        add_into(f.xs, 2 * TB, 96, [f.r2])
-        start(f.t2l)
-
-    def back_0(f):
-        project_back(f, 0)
+        start(f.t1b)
+
+    def add_1x(f):
         got(f.t5r, f.t4l)
-        add_into(f.xs, TB, 64, [f.la1, f.ra1])
-        start(f.t1z)
-
-    def finish(f):
-        got(f.t3r, f.t2l, f.t1z)
-
-        @pl.loop(0, 8)
+        add_into(f.xs, TB, CUT, [f.la1, f.ra1])
+        start(f.t1a)
+
+    def finish(f, lo, n, srcs, hop):
+        @pl.loop(0, n // 16)
         def _(i):
-            r = pl.ds(pl.multiple_of(i * 16, 16), 16)
+            at = pl.multiple_of(i * 16, 16)
+            r = pl.ds(lo + at, 16)
             total = f.xs[r, :].astype(F32) + f.x[r, :].astype(F32)
-            for src in (f.l0, f.r0, f.z0):
-                total = total + src[r, :].astype(F32)
+            for src in srcs:
+                total = total + src[pl.ds(at, 16), :].astype(F32)
             f.out[r, :] = total.astype(BF16)
 
-        start(f.hop)
-
-    send_own(fb)
+        start(hop)
+
+    def finish_high(f):
+        got(f.t3a, f.t2a, f.t1a)
+        finish(f, 0, CUT, (f.l0a, f.r0a, f.z0a), f.hops[0])
+
+    def finish_low(f):
+        got(f.t3b, f.t2b, f.t1b)
+        finish(f, CUT, LOW, (f.l0b, f.r0b, f.z0b), f.hops[1])
+
+    send_own(ff)
     make_bias()
+    wq_load.wait()
+    order_weights()
+    for copy in own_loads + wo_loads:
+        copy.wait()
+    project(ff, 0)
+    pass_low(ff)
     for copy in sv_loads:
         copy.wait()
-    saved_probs()
-    for copy in own_loads + wo_loads:
-        copy.wait()
-    forward_near(fb)
-    project(fb, 0)
-    forward_far(fb)
-    send_own(ff)
-    project(fb, 1)
-    sum_two(fb, 0)
-    wq_load.wait()
-    order_weights()
-    got(fb.z_r, fb.fwd_z2, fb.fwd_z3)
-    project(fb, 2)
-    sum_two(fb, 1)
-    sum_all(fb, 0)
-    got(fb.z_l2, fb.far_a, fb.far_b)
-    project(fb, 3)
-    sum_two(fb, 2)
-    sum_all(fb, 1)
-    forward_near(ff)
-    sum_two(fb, 3)
-    sum_all(fb, 2)
-    project(ff, 0)
-    sum_all(fb, 3)
-    backward_head()
-    for g in (3, 2, 1, 0):
-        heads_out(fb, g)
-    forward_far(ff)
+    saved_probs(0)
+    sum_two(ff, 0)
+    saved_probs(1)
+    pass_high(ff)
+    near_here(ff)
     project(ff, 1)
-    sum_two(ff, 0)
-    heads_on(fb, 3)
-    got(ff.z_r, ff.fwd_z2, ff.fwd_z3)
+    pass_far_low(ff)
     project(ff, 2)
+    pass_far_high(ff)
+    send_own(fb)
+    sum_all(ff, 0)
     sum_two(ff, 1)
-    heads_on(fb, 2)
-    got(ff.z_l2, ff.far_a, ff.far_b)
+    diagonal_here(ff)
     project(ff, 3)
     sum_two(ff, 2)
-    sum_all(ff, 0)
+    sum_all(ff, 1)
+    far_here(ff)
+    project(ff, 4)
+    sum_two(ff, 3)
+    saved_probs(2)
+    sum_all(ff, 2)
+    pass_low(fb)
+    sum_two(ff, 4)
+    saved_probs(3)
+    project(fb, 0)
+    pass_high(fb)
+    near_here(fb)
+    project(fb, 1)
+    project(fb, 2)
+    sum_all(ff, 3)
+    pass_far_low(fb)
+    sum_two(fb, 0)
+    sum_two(fb, 1)
+    pass_far_high(fb)
+    sum_all(ff, 4)
+    forward_head(4)
+    heads_out(ff, 4)
+    sum_two(fb, 2)
+    forward_head(3)
+    heads_out(ff, 3)
+    diagonal_here(fb)
+    project(fb, 3)
+    heads_on(ff, 4)
+    forward_head(2)
+    heads_out(ff, 2)
+    heads_on(ff, 3)
+    far_here(fb)
+    project(fb, 4)
+    sum_two(fb, 3)
+    back_4(ff)
+    forward_head(1)
+    heads_out(ff, 1)
+    forward_head(0)
+    heads_out(ff, 0)
+    heads_on(ff, 2)
+    sum_two(fb, 4)
+    sum_all(fb, 0)
+    sum_all(fb, 1)
+    sum_all(fb, 2)
+    back_3(ff)
+    add_4z(ff)
+    heads_on(ff, 1)
+    heads_on(ff, 0)
+    sum_all(fb, 3)
+    sum_all(fb, 4)
+    backward_head()
+    heads_out(fb, 4)
+    heads_out(fb, 3)
+    add_3x(ff)
+    back_2(ff)
+    add_2x(ff)
+    back_1(ff)
+    heads_on(fb, 4)
+    heads_out(fb, 2)
+    add_1x(ff)
+    add_2z(ff)
+    project_back(ff, 0)
+    heads_on(fb, 3)
+    heads_out(fb, 1)
+    heads_out(fb, 0)
+    back_4(fb)
+    finish_high(ff)
+    finish_low(ff)
+    heads_on(fb, 2)
+    add_4z(fb)
+    back_3(fb)
+    add_3x(fb)
     heads_on(fb, 1)
-    back_3(fb)
-    sum_two(ff, 3)
-    sum_all(ff, 1)
     heads_on(fb, 0)
     back_2(fb)
-    sum_all(ff, 2)
-    sum_all(ff, 3)
-    for g in (3, 2, 1, 0):
-        forward_head(g)
-        heads_out(ff, g)
+    add_2x(fb)
     back_1(fb)
-    heads_on(ff, 3)
-    heads_on(ff, 2)
-    back_0(fb)
-    heads_on(ff, 1)
-    heads_on(ff, 0)
-    back_3(ff)
-    back_2(ff)
-    finish(fb)
-    back_1(ff)
-    back_0(ff)
-    finish(ff)
-    got(fb.hop, ff.hop)
+    add_1x(fb)
+    add_2z(fb)
+    project_back(fb, 0)
+    finish_high(fb)
+    finish_low(fb)
+    got(*fb.hops, *ff.hops)
     for copy in sent:
         copy.wait_send()
     assert len(sent) <= N_SEMS
+
+
+def hand_over(a, b, a_out, b_out):
+    a_out[...] = a[...]
+    b_out[...] = b[...]
 
 
 def per_device(fwd_input, grad_out, w_qkv, w_out, saved_qkv, rand_blocks):
@@ -409,7 +515,7 @@
             vmem(16, 8, T, dtype=F32), vmem(T, T), vmem(T, HD),
             *pair(T, 512, 1536), *pair(512, 128, 384), *pair(512, 128, 384), *pair(T, 128, 384), *pair(T, 128, 384),
             *pair(T, 128, 384), vmem(T, HD, dtype=F32), vmem(T, HD, dtype=F32), vmem(T, 512), vmem(T, 1536),
-            *pair(T, W, W), *pair(320, W, W), *pair(288, W, W), *pair(288, W, W), *pair(TB, W, W),
+            *pair(T, W, W), *pair(TB + 3 * LOW, W, W), *pair(TB + 2 * CUT + TB - MID, W, W), *pair(TB + CUT + MID, W, W), *pair(TB, W, W),
             pltpu.SemaphoreType.DMA((16,)), pltpu.SemaphoreType.DMA((N_SEMS,)), pltpu.SemaphoreType.DMA((N_SEMS,)),
         ],
         compiler_params=pltpu.CompilerParams(
@@ -422,8 +528,16 @@
         w_qkv.reshape(12 * W, HD),
         w_out.reshape(512, W),
         saved_qkv.reshape(3, T, HD),
-        rand_blocks.reshape(16, 3),
+        rand_blocks.transpose(0, 3, 1, 2).reshape(3, 1, 16),
     )
+    block = pl.BlockSpec((TB // 2, W), lambda i: (i, 0))
+    fwd_next, grad_prev = pl.pallas_call(
+        hand_over,
+        grid=(2,),
+        out_shape=[jax.ShapeDtypeStruct((TB, W), BF16)] * 2,
+        in_specs=[block] * 2,
+        out_specs=[block] * 2,
+    )(fwd_next, grad_prev)
     return (fwd_next[None], grad_prev[None])
 
 

time: 160 us -> 131 us (0.82)
  the two profiles are of different devices: /device:TPU:161 before, /device:TPU:65 now
where the time goes in v2:
time: 131 us; the launch traced here: 129 us
  Pallas kernels  128 us (98%)
    pallas_call x1, Pallas kernels, per_device(): pl.pallas_call(kernel, out_shape=[jax.ShapeDtypeStruct((TB, W), BF16)] *...  126 us

profile of v2, /device:TPU:65, one launch (start us, length us, event | category | flops | bytes accessed | tf_op | source)
XLA Modules:
  0.0 128.7 jit_solution(15054527731349019353)
XLA Ops:
  0.6 126.1 %shard_map.77 = (bf16[128,1536]{1,0:T(8,128)(2,1)}, bf16[128,1536]{1,0:T(8,128)(2,1)}) custom-call(bf16[128,1536]{1,0:T(8,128)(2,1)} %bitcast.13, bf16[128,1536]{1,0:T(8,128)(2,1)} %bitcast.14, bf16[18432,128]{1,0:T(8,128)(2,1)} %bitcast.10, bf16[512,1536]{1,0:T(8,128)(2,1)} %bitcast.11, bf16[3,1024,128]{2,1,0:T(8,128)(2,1)} %bitcast.12, s32[3,1,16]{2,1,0:T(1,128)} %bitcast.17), custom_call_target="tpu_custom_call" | custom-call | flops 16000000000 | bytes 10000000 | tf_op jit(solution)/shard_map/pallas_call | solution.py:508
  126.7 2.0 %shard_map.78 = (bf16[128,1536]{1,0:T(8,128)(2,1)}, bf16[128,1536]{1,0:T(8,128)(2,1)}) custom-call(bf16[128,1536]{1,0:T(8,128)(2,1)} %get-tuple-element.6.a, bf16[128,1536]{1,0:T(8,128)(2,1)} %get-tuple-element.7.b), custom_call_target="tpu_custom_call" | custom-call | tf_op jit(solution)/shard_map/pallas_call | solution.py:534

commit v3 on v2

--- a/solution.py
+++ b/solution.py
@@ -11,10 +11,19 @@
 F32, BF16 = jnp.float32, jnp.bfloat16
 T, TB, W, HD = 1024, 128, 1536, 128
 PLACES = ((0, 0), (0, 1), (-1, 0), (1, 0), (-1, 1), (1, 1), (2, 0), (2, 1))
-GROUPS = ((0, 1), (1, 1), (2, 2), (4, 2), (6, 2))
+ORDER = (
+    (0, 0), (0, 1), (2, 1), (3, 1), (1, 0), (2, 0), (3, 0), (1, 1),
+    (6, 1), (4, 1), (4, 0), (5, 0), (5, 1), (6, 0), (7, 0), (7, 1),
+)
+ROW = {block: 64 * i for i, block in enumerate(ORDER)}
+GROUPS = (
+    ((0, 2), (2, 3), (5, 3), (8, 4), (12, 4)),
+    ((0, 2), (2, 3), (5, 3), (8, 2), (10, 2), (12, 2), (14, 2)),
+)
+RESULTS = ((0, 2), (2, 2), (4, 3), (7, 1), (8, 4), (12, 2), (14, 2))
 CUT, MID = 64, 96
 LOW = TB - CUT
-N_SEMS = 160
+N_SENT, N_SEMS = 64, 190
 
 
 def nn(a, b):
@@ -54,8 +63,11 @@
         return copy
 
     sv_loads = [
-        load(sv_in.at[:, pl.ds(pl.multiple_of(owner[s] * TB, TB), TB), :], sv.at[:, pl.ds(s * TB, TB), :])
-        for s in range(8)
+        load(
+            sv_in.at[:, pl.ds(pl.multiple_of(owner[s] * TB + half * 64, 64), 64), :],
+            sv.at[:, pl.ds(ROW[s, half], 64), :],
+        )
+        for s, half in ORDER
     ]
     own_loads = [load(gout, x_b.at[pl.ds(0, TB)]), load(fin, x_f.at[pl.ds(0, TB)])]
     wo_loads = [
@@ -69,19 +81,29 @@
         pl.semaphore_signal(barrier, inc=1, device_id=other, device_id_type=MESH)
     pl.semaphore_wait(barrier, 7)
 
-    sent = []
+    count, pending, free = [0], [], list(range(N_SENT))
+
+    class Message:
+        def __init__(self, src, dst, other):
+            self.ends = (src, dst, other)
+            self.k = count[0]
+            count[0] += 1
+
+        def copy(self, slot):
+            src, dst, other = self.ends
+            return pltpu.make_async_remote_copy(
+                src_ref=src, dst_ref=dst, send_sem=send_sem.at[slot], recv_sem=recv_sem.at[self.k],
+                device_id=other, device_id_type=MESH,
+            )
 
     def msg(src, dst, other):
-        k = len(sent)
-        copy = pltpu.make_async_remote_copy(
-            src_ref=src, dst_ref=dst, send_sem=send_sem.at[k], recv_sem=recv_sem.at[k],
-            device_id=other, device_id_type=MESH,
-        )
-        sent.append(copy)
-        return copy
-
-    def part(ref, s, lo=0, hi=TB):
-        return ref.at[pl.ds(s * TB + lo, hi - lo)]
+        return Message(src, dst, other)
+
+    def row(s, lo):
+        return ROW[s, lo // CUT] + lo % CUT
+
+    def part(ref, s, lo, hi):
+        return ref.at[pl.ds(row(s, lo), hi - lo)]
 
     class Flow:
         pass
@@ -110,20 +132,33 @@
         f.z_l2 = msg(part(x, 5, 0, CUT), part(x, 7, 0, CUT), left)
         f.far_a = msg(part(x, 6, CUT, MID), part(x, 7, CUT, MID), across)
         f.far_b = msg(part(x, 6, MID, TB), part(x, 7, MID, TB), across)
-        f.s2u, f.s2d, f.s1u, f.s1d, f.hu, f.hd, f.h2u, f.h2d = [], [], [], [], [], [], [], []
-        v = 512 - w
-        f.v = v
-        for at, n in GROUPS:
-            all_rows, half = pl.ds(at * TB, n * TB), pl.ds(at * TB // 2, n * TB // 2)
-            first, last = pl.ds(at * TB, n * TB // 2), pl.ds(at * TB + n * TB // 2, n * TB // 2)
+        f.s2u, f.s2d, f.s1u, f.s1d = [], [], [], []
+        f.groups = GROUPS[w == 384]
+        for at, n in f.groups:
+            all_rows, half = pl.ds(at * 64, n * 64), pl.ds(at * 32, n * 32)
+            first, last = pl.ds(at * 64, n * 32), pl.ds(at * 64 + n * 32, n * 32)
             f.s2u.append(msg(yp.at[first, pl.ds(2 * w, w)], y2u.at[half], up))
             f.s2d.append(msg(yp.at[last, pl.ds(2 * w, w)], y2d.at[half], down))
             f.s1u.append(msg(yp.at[all_rows, pl.ds(w, w)], ya.at[all_rows], up))
             f.s1d.append(msg(yp.at[all_rows, pl.ds(3 * w, w)], yb.at[all_rows], down))
-            f.hu.append(msg(heads.at[all_rows, pl.ds(0, v)], heads.at[all_rows, pl.ds(3 * v, v)], up))
-            f.hd.append(msg(heads.at[all_rows, pl.ds(0, v)], heads.at[all_rows, pl.ds(v, v)], down))
-            f.h2u.append(msg(heads.at[first, pl.ds(3 * v, v)], heads.at[first, pl.ds(2 * v, v)], up))
-            f.h2d.append(msg(heads.at[last, pl.ds(v, v)], heads.at[last, pl.ds(2 * v, v)], down))
+
+        def round_y(groups, at_col, v):
+            hu, hd, h2u, h2d = [], [], [], []
+            for at, n in groups:
+                all_rows = pl.ds(at * 64, n * 64)
+                first, last = pl.ds(at * 64, n * 32), pl.ds(at * 64 + n * 32, n * 32)
+                c = [pl.ds(heads.shape[1] // 4 * j + at_col, v) for j in range(4)]
+                hu.append(msg(heads.at[all_rows, c[0]], heads.at[all_rows, c[3]], up))
+                hd.append(msg(heads.at[all_rows, c[0]], heads.at[all_rows, c[1]], down))
+                h2u.append(msg(heads.at[first, c[3]], heads.at[first, c[2]], up))
+                h2d.append(msg(heads.at[last, c[1]], heads.at[last, c[2]], down))
+            return hu, hd, h2u, h2d
+
+        if w == 384:
+            f.results = round_y(RESULTS, 0, HD)
+        else:
+            f.results = round_y(RESULTS, HD, 2 * HD)
+            f.queries = round_y(f.groups, 0, HD)
         def cuts(ref, *sizes):
             at = [sum(sizes[:i]) for i in range(len(sizes))]
             return [ref.at[pl.ds(lo, n)] for lo, n in zip(at, sizes)]
@@ -143,13 +178,24 @@
         flows.append(f)
     fb, ff = flows
 
-    def start(*copies):
-        for copy in copies:
+    def drain(n):
+        for copy, slot in pending[:n]:
+            copy.wait_send()
+            free.append(slot)
+        del pending[:n]
+
+    def start(*messages):
+        for message in messages:
+            if not free:
+                drain(8)
+            slot = free.pop(0)
+            copy = message.copy(slot)
             copy.start()
-
-    def got(*copies):
-        for copy in copies:
-            copy.wait_recv()
+            pending.append((copy, slot))
+
+    def got(*messages):
+        for message in messages:
+            message.copy(0).wait_recv()
 
     def send_own(f):
         start(f.own_z[0], f.own_r[1], f.own_l[1], f.own_z[1], f.own_r[0], f.own_l[0])
@@ -178,10 +224,10 @@
         got(f.own_z[1], f.own_l[0])
 
     def diagonal_here(f):
-        got(f.z_r, f.fwd_z2, f.fwd_z3)
+        got(f.z_r, f.fwd_z2)
 
     def far_here(f):
-        got(f.fwd_r, f.z_l2, f.far_a, f.far_b)
+        got(f.fwd_z3, f.fwd_r, f.z_l2, f.far_a, f.far_b)
 
     def add_into(dst, lo, n, srcs, cols=None):
         @pl.loop(0, n // 16)
@@ -193,13 +239,13 @@
                 total = total + src[pl.ds(pl.multiple_of(i * 16, 16), 16), :].astype(F32)
             dst[r, c] = total.astype(BF16)
 
-    def rows_of(g):
-        return pl.ds(GROUPS[g][0] * TB, GROUPS[g][1] * TB)
+    def rows_of(f, g):
+        return pl.ds(f.groups[g][0] * 64, f.groups[g][1] * 64)
 
     def project(f, g):
-        r = rows_of(g)
-
-        @pl.loop(0, 4 * f.w // 256)
+        r = rows_of(f, g)
+
+        @pl.loop(0, 4 * f.w // 256, unroll=min(3, 4 * f.w // 256))
         def _(n):
             c = pl.ds(pl.multiple_of(n * 256, 256), 256)
             p = nn(f.x[r, :], wp[:, c]) if f is ff else nt(f.x[r, :], wo[c, :])
@@ -208,7 +254,7 @@
         start(f.s2u[g], f.s2d[g])
 
     def sum_two(f, g):
-        at, n = GROUPS[g][0] * TB, GROUPS[g][1] * TB // 2
+        at, n = f.groups[g][0] * 64, f.groups[g][1] * 32
         got(f.s2u[g])
         add_into(f.yp, at, n, [f.y2u.at[pl.ds(at // 2, n)]], pl.ds(f.w, f.w))
         start(f.s1u[g])
@@ -219,25 +265,25 @@
     def sum_all(f, g):
         got(f.s1u[g], f.s1d[g])
 
-        @pl.loop(0, GROUPS[g][1] * 8)
+        @pl.loop(0, f.groups[g][1] * 4)
         def _(i):
-            r = pl.ds(GROUPS[g][0] * TB + pl.multiple_of(i * 16, 16), 16)
+            r = pl.ds(f.groups[g][0] * 64 + pl.multiple_of(i * 16, 16), 16)
             total = f.yp[r, pl.ds(0, f.w)].astype(F32) + f.ya[r, :].astype(F32) + f.yb[r, :].astype(F32)
             f.act[r, :] = total.astype(BF16)
 
     def make_bias():
         lane = lax.broadcasted_iota(jnp.int32, (8, T), 1)
-        key = lane // 64 % 2
-        for s in range(8):
-            key = key + jnp.where(lane // TB == s, 2 * owner[s], 0)
-        for s in range(8):
-            for half in range(2):
-                q = 2 * owner[s] + half
-                ok = (key < 2) | (key == q) | (key == (q + 1) % 16) | (key == (q + 15) % 16)
-                for n in range(3):
-                    ok = ok | (key == rnd[n, 0, q])
-                ok = ok | (jnp.full((8, T), q, jnp.int32) < 2)
-                bias[2 * s + half] = jnp.where(ok, 0.0, -1e30).astype(F32)
+        lane_block = lane // 64
+        key = jnp.zeros((8, T), jnp.int32)
+        for i, (s, half) in enumerate(ORDER):
+            key = jnp.where(lane_block == i, 2 * owner[s] + half, key)
+        for i, (s, half) in enumerate(ORDER):
+            q = 2 * owner[s] + half
+            ok = (key < 2) | (key == q) | (key == (q + 1) % 16) | (key == (q + 15) % 16)
+            for n in range(3):
+                ok = ok | (key == rnd[n, 0, q])
+            ok = ok | (jnp.full((8, T), q, jnp.int32) < 2)
+            bias[i] = jnp.where(ok, 0.0, -1e30).astype(F32)
 
     def softmax(q, k, b0):
         n = q.shape[0] // 64
@@ -254,39 +300,55 @@
             probs[r, :] = p
             head_out[r, :] = nn(p, sv[2]).astype(BF16)
 
-    def backward_head():
+    def backward_start():
         dk[...] = jnp.zeros_like(dk)
         dv[...] = jnp.zeros_like(dv)
 
-        @pl.loop(0, 4)
-        def _(i):
-            r = pl.ds(pl.multiple_of(i * 256, 256), 256)
-            g = act_b[r, :]
-            delta = jnp.sum(g.astype(F32) * head_out[r, :].astype(F32), axis=-1, keepdims=True)
-            p = probs[r, :]
-            ds = (p.astype(F32) * (nt(g, sv[2]) - delta)).astype(BF16)
-            grads[r, pl.ds(0, HD)] = (nn(ds, sv[1]) * scale).astype(BF16)
-            dk[...] += tn(ds, sv[0, r, :])
-            dv[...] += tn(p, g)
-
+    def backward_rows(g):
+        r = rows_of(fb, g)
+        grad = act_b[r, :]
+        delta = jnp.sum(grad.astype(F32) * head_out[r, :].astype(F32), axis=-1, keepdims=True)
+        p = probs[r, :]
+        ds = (p.astype(F32) * (nt(grad, sv[2]) - delta)).astype(BF16)
+        grads[r, pl.ds(0, HD)] = (nn(ds, sv[1]) * scale).astype(BF16)
+        start(fb.queries[0][g], fb.queries[1][g])
+        dk[...] += tn(ds, sv[0, r, :])
+        dv[...] += tn(p, grad)
+
+    def queries_on(g):
+        got(fb.queries[0][g])
+        start(fb.queries[2][g])
+        got(fb.queries[1][g])
+        start(fb.queries[3][g])
+
+    def queries_here(*groups):
+        for g in groups:
+            got(fb.queries[2][g], fb.queries[3][g])
+
+    def backward_end():
         grads[:, pl.ds(HD, HD)] = (dk[...] * scale).astype(BF16)
         grads[:, pl.ds(2 * HD, HD)] = dv[...].astype(BF16)
 
     def forward_head(g):
-        @pl.loop(0, GROUPS[g][1])
+        at, n = RESULTS[g]
+        size = 128 if n % 2 == 0 else n * 64
+
+        @pl.loop(0, n * 64 // size)
         def _(i):
-            r = pl.ds(GROUPS[g][0] * TB + pl.multiple_of(i * TB, TB), TB)
-            p = softmax(act_f[r, pl.ds(0, HD)], act_f[:, pl.ds(HD, HD)], (GROUPS[g][0] + i) * 2)
+            r = pl.ds(at * 64 + pl.multiple_of(i * size, 64), size)
+            p = softmax(act_f[r, pl.ds(0, HD)], act_f[:, pl.ds(HD, HD)], at + i * (size // 64))
             mixed[r, pl.ds(0, HD)] = nn(p, act_f[:, pl.ds(2 * HD, HD)]).astype(BF16)
 
+        start(ff.results[0][g], ff.results[1][g])
+
     def heads_out(f, g):
-        start(f.hu[g], f.hd[g])
+        start(f.results[0][g], f.results[1][g])
 
     def heads_on(f, g):
-        got(f.hu[g])
-        start(f.h2u[g])
-        got(f.hd[g])
-        start(f.h2d[g])
+        got(f.results[0][g])
+        start(f.results[2][g])
+        got(f.results[1][g])
+        start(f.results[3][g])
 
     def order_weights():
         row, col = lax.broadcasted_iota(jnp.int32, (256, 256), 0), lax.broadcasted_iota(jnp.int32, (256, 256), 1)
@@ -304,60 +366,63 @@
                         )
 
     def project_back(f, g):
-        got(f.h2u[g], f.h2d[g])
-        r = rows_of(g)
-
-        @pl.loop(0, 6)
+        got(f.results[2][g], f.results[3][g])
+        r = pl.ds(RESULTS[g][0] * 64, RESULTS[g][1] * 64)
+
+        @pl.loop(0, 6, unroll=3)
         def _(n):
             c = pl.ds(pl.multiple_of(n * 256, 256), 256)
             p = nn(f.heads[r, :], wo[:, c]) if f is ff else nt(f.heads[r, :], wp[c, :])
             f.xs[r, c] = p.astype(BF16)
 
+    def back_6(f):
+        project_back(f, 6)
+        start(f.t7z, f.t7r)
+
+    def back_5(f):
+        project_back(f, 5)
+        start(f.t6l, f.t5z)
+
     def back_4(f):
         project_back(f, 4)
-        start(f.t7z, f.t7r, f.t6l)
-
-    def add_4z(f):
+        start(f.t4l, f.t4z)
+
+    def add_6(f):
         got(f.t7z)
-        add_into(f.xs, 6 * TB + CUT, LOW, [f.zb6])
+        add_into(f.xs, row(6, CUT), LOW, [f.zb6])
         start(f.t6q, f.t6r)
+
+    def add_5(f):
+        got(f.t7r)
+        add_into(f.xs, row(5, 0), CUT, [f.la5])
+        start(f.t5r)
 
     def back_3(f):
         project_back(f, 3)
-        start(f.t5z, f.t4z, f.t4l)
-
-    def add_3x(f):
-        got(f.t7r)
-        add_into(f.xs, 5 * TB, CUT, [f.la5])
-        start(f.t5r)
+        start(f.t1b)
 
     def back_2(f):
         project_back(f, 2)
         start(f.t3a)
-
-    def add_2x(f):
         got(f.t6l)
-        add_into(f.xs, 2 * TB, CUT, [f.r2a])
+        add_into(f.xs, row(2, 0), CUT, [f.r2a])
         start(f.t2a)
 
-    def add_2z(f):
+    def add_1(f):
+        got(f.t5r, f.t4l)
+        add_into(f.xs, row(1, 0), CUT, [f.la1, f.ra1])
+        start(f.t1a)
+
+    def back_1(f):
+        project_back(f, 1)
         got(f.t5z, f.t6r)
-        add_into(f.xs, 3 * TB + CUT, LOW, [f.zb3])
-        add_into(f.xs, 3 * TB + MID, TB - MID, [f.l3])
+        add_into(f.xs, row(3, CUT), LOW, [f.zb3])
+        add_into(f.xs, row(3, MID), TB - MID, [f.l3])
         start(f.t3b)
         got(f.t4z, f.t6q)
-        add_into(f.xs, 2 * TB + CUT, LOW, [f.zb2])
-        add_into(f.xs, 2 * TB + CUT, MID - CUT, [f.r2q])
+        add_into(f.xs, row(2, CUT), LOW, [f.zb2])
+        add_into(f.xs, row(2, CUT), MID - CUT, [f.r2q])
         start(f.t2b)
-
-    def back_1(f):
-        project_back(f, 1)
-        start(f.t1b)
-
-    def add_1x(f):
-        got(f.t5r, f.t4l)
-        add_into(f.xs, TB, CUT, [f.la1, f.ra1])
-        start(f.t1a)
 
     def finish(f, lo, n, srcs, hop):
         @pl.loop(0, n // 16)
@@ -387,109 +452,135 @@
         copy.wait()
     project(ff, 0)
     pass_low(ff)
+    project(ff, 1)
+    sum_two(ff, 0)
+    pass_high(ff)
+    near_here(ff)
+    project(ff, 2)
+    pass_far_low(ff)
+    sum_two(ff, 1)
+    sum_all(ff, 0)
     for copy in sv_loads:
         copy.wait()
     saved_probs(0)
-    sum_two(ff, 0)
-    saved_probs(1)
-    pass_high(ff)
-    near_here(ff)
-    project(ff, 1)
-    pass_far_low(ff)
-    project(ff, 2)
     pass_far_high(ff)
     send_own(fb)
-    sum_all(ff, 0)
-    sum_two(ff, 1)
-    diagonal_here(ff)
+    sum_two(ff, 2)
+    got(ff.fwd_z2)
     project(ff, 3)
-    sum_two(ff, 2)
+    got(ff.z_r)
+    project(ff, 4)
     sum_all(ff, 1)
-    far_here(ff)
-    project(ff, 4)
     sum_two(ff, 3)
-    saved_probs(2)
+    got(ff.fwd_z3, ff.fwd_r)
+    project(ff, 5)
+    sum_two(ff, 4)
+    got(ff.z_l2, ff.far_a, ff.far_b)
+    project(ff, 6)
     sum_all(ff, 2)
     pass_low(fb)
-    sum_two(ff, 4)
-    saved_probs(3)
+    sum_two(ff, 5)
     project(fb, 0)
+    project(fb, 1)
+    sum_two(ff, 6)
+    sum_all(ff, 3)
+    saved_probs(1)
     pass_high(fb)
     near_here(fb)
-    project(fb, 1)
     project(fb, 2)
-    sum_all(ff, 3)
     pass_far_low(fb)
+    sum_all(ff, 4)
     sum_two(fb, 0)
+    saved_probs(2)
+    sum_all(ff, 5)
     sum_two(fb, 1)
+    sum_all(ff, 6)
+    forward_head(6)
     pass_far_high(fb)
-    sum_all(ff, 4)
+    forward_head(5)
+    sum_two(fb, 2)
     forward_head(4)
-    heads_out(ff, 4)
-    sum_two(fb, 2)
-    forward_head(3)
-    heads_out(ff, 3)
+    heads_on(ff, 6)
     diagonal_here(fb)
     project(fb, 3)
-    heads_on(ff, 4)
+    forward_head(3)
     forward_head(2)
-    heads_out(ff, 2)
-    heads_on(ff, 3)
+    heads_on(ff, 5)
+    sum_two(fb, 3)
+    forward_head(1)
+    forward_head(0)
+    back_6(ff)
     far_here(fb)
     project(fb, 4)
-    sum_two(fb, 3)
-    back_4(ff)
-    forward_head(1)
-    heads_out(ff, 1)
-    forward_head(0)
-    heads_out(ff, 0)
-    heads_on(ff, 2)
-    sum_two(fb, 4)
+    heads_on(ff, 4)
     sum_all(fb, 0)
     sum_all(fb, 1)
+    back_5(ff)
+    sum_two(fb, 4)
+    saved_probs(3)
+    backward_start()
+    backward_rows(0)
+    backward_rows(1)
+    heads_on(ff, 3)
+    heads_on(ff, 2)
     sum_all(fb, 2)
-    back_3(ff)
-    add_4z(ff)
+    backward_rows(2)
+    back_4(ff)
+    add_6(ff)
+    add_5(ff)
+    sum_all(fb, 3)
+    backward_rows(3)
+    sum_all(fb, 4)
+    backward_rows(4)
+    backward_end()
+    heads_out(fb, 6)
+    heads_out(fb, 5)
     heads_on(ff, 1)
     heads_on(ff, 0)
-    sum_all(fb, 3)
-    sum_all(fb, 4)
-    backward_head()
+    queries_on(0)
+    queries_on(1)
+    queries_on(2)
+    back_3(ff)
+    queries_on(3)
+    queries_on(4)
+    heads_on(fb, 6)
     heads_out(fb, 4)
+    back_2(ff)
+    add_1(ff)
+    heads_on(fb, 5)
+    back_1(ff)
     heads_out(fb, 3)
-    add_3x(ff)
-    back_2(ff)
-    add_2x(ff)
-    back_1(ff)
+    heads_out(fb, 2)
+    queries_here(4)
+    back_6(fb)
     heads_on(fb, 4)
-    heads_out(fb, 2)
-    add_1x(ff)
-    add_2z(ff)
-    project_back(ff, 0)
-    heads_on(fb, 3)
     heads_out(fb, 1)
     heads_out(fb, 0)
-    back_4(fb)
+    project_back(ff, 0)
+    back_5(fb)
     finish_high(ff)
     finish_low(ff)
+    queries_here(3)
+    back_4(fb)
+    add_6(fb)
+    add_5(fb)
+    heads_on(fb, 3)
     heads_on(fb, 2)
-    add_4z(fb)
+    queries_here(2)
     back_3(fb)
-    add_3x(fb)
     heads_on(fb, 1)
     heads_on(fb, 0)
+    queries_here(1)
     back_2(fb)
-    add_2x(fb)
+    add_1(fb)
     back_1(fb)
-    add_1x(fb)
-    add_2z(fb)
+    queries_here(0)
     project_back(fb, 0)
     finish_high(fb)
     finish_low(fb)
     got(*fb.hops, *ff.hops)
-    for copy in sent:
-        copy.wait_send()
-    assert len(sent) <= N_SEMS
+    drain(len(pending))
+    assert count[0] == N_SEMS, count
 
 
 def hand_over(a, b, a_out, b_out):
@@ -516,7 +607,7 @@
             *pair(T, 512, 1536), *pair(512, 128, 384), *pair(512, 128, 384), *pair(T, 128, 384), *pair(T, 128, 384),
             *pair(T, 128, 384), vmem(T, HD, dtype=F32), vmem(T, HD, dtype=F32), vmem(T, 512), vmem(T, 1536),
             *pair(T, W, W), *pair(TB + 3 * LOW, W, W), *pair(TB + 2 * CUT + TB - MID, W, W), *pair(TB + CUT + MID, W, W), *pair(TB, W, W),
-            pltpu.SemaphoreType.DMA((16,)), pltpu.SemaphoreType.DMA((N_SEMS,)), pltpu.SemaphoreType.DMA((N_SEMS,)),
+            pltpu.SemaphoreType.DMA((24,)), pltpu.SemaphoreType.DMA((N_SENT,)), pltpu.SemaphoreType.DMA((N_SEMS,)),
         ],
         compiler_params=pltpu.CompilerParams(
             collective_id=0, has_side_effects=True, vmem_limit_bytes=62 * 1024 * 1024

time: 131 us -> 122 us (0.931); the launches traced: 129 us -> 121 us
  Pallas kernels: 128 us -> 121 us
    pallas_call x1, Pallas kernels: 126 us -> 119 us  [per_device(): pl.pallas_call(kernel, out_shape=[jax.ShapeDtypeStruct((TB, W), BF16)] *...]
where the time goes in v3:
time: 122 us; the launch traced here: 121 us
  Pallas kernels  121 us (99%)
    pallas_call x1, Pallas kernels, per_device(): pl.pallas_call(kernel, out_shape=[jax.ShapeDtypeStruct((TB, W), BF16)] *...  119 us

profile of v3, /device:TPU:65, one launch (start us, length us, event | category | flops | bytes accessed | tf_op | source)
XLA Modules:
  0.0 121.4 jit_solution(16196856760682331831)
XLA Ops:
  0.6 118.8 %shard_map.77 = (bf16[128,1536]{1,0:T(8,128)(2,1)}, bf16[128,1536]{1,0:T(8,128)(2,1)}) custom-call(bf16[128,1536]{1,0:T(8,128)(2,1)} %bitcast.13, bf16[128,1536]{1,0:T(8,128)(2,1)} %bitcast.14, bf16[18432,128]{1,0:T(8,128)(2,1)} %bitcast.10, bf16[512,1536]{1,0:T(8,128)(2,1)} %bitcast.11, bf16[3,1024,128]{2,1,0:T(8,128)(2,1)} %bitcast.12, s32[3,1,16]{2,1,0:T(1,128)} %bitcast.17), custom_call_target="tpu_custom_call" | custom-call | flops 16000000000 | bytes 10000000 | tf_op jit(solution)/shard_map/pallas_call | solution.py:599
  119.4 2.0 %shard_map.78 = (bf16[128,1536]{1,0:T(8,128)(2,1)}, bf16[128,1536]{1,0:T(8,128)(2,1)}) custom-call(bf16[128,1536]{1,0:T(8,128)(2,1)} %get-tuple-element.6.a, bf16[128,1536]{1,0:T(8,128)(2,1)} %get-tuple-element.7.b), custom_call_target="tpu_custom_call" | custom-call | tf_op jit(solution)/shard_map/pallas_call | solution.py:625

commit v4 on v3

--- a/solution.py
+++ b/solution.py
@@ -1,4 +1,6 @@
+import functools
 import math
+import types
 
 import jax
 import jax.numpy as jnp
@@ -21,9 +23,9 @@
     ((0, 2), (2, 3), (5, 3), (8, 2), (10, 2), (12, 2), (14, 2)),
 )
 RESULTS = ((0, 2), (2, 2), (4, 3), (7, 1), (8, 4), (12, 2), (14, 2))
-CUT, MID = 64, 96
+CUT, MID, SIDE = 64, 96, 112
 LOW = TB - CUT
-N_SENT, N_SEMS = 64, 190
+N_SENT, N_SEMS = 64, 198
 
 
 def nn(a, b):
@@ -40,7 +42,7 @@
 
 def kernel(fin, gout, wq, wo_in, sv_in, rnd, fnext, gprev, x_b, x_f, w_raw, wp, wo, sv, bias, probs, head_out,
            yp_b, yp_f, y2u_b, y2u_f, y2d_b, y2d_f, ya_b, ya_f, yb_b, yb_f, act_b, act_f, dk, dv, mixed, grads,
-           xs_b, xs_f, rz_b, rz_f, rl_b, rl_f, rr_b, rr_f, out_b, out_f, load_sem, send_sem, recv_sem):
+           xs_b, xs_f, rz_b, rz_f, rl_b, rl_f, rr_b, rr_f, out_b, out_f, pick, wpt, load_sem, send_sem, recv_sem):
     sec, ctx, tp = lax.axis_index("section"), lax.axis_index("ctx"), lax.axis_index("tp")
     zl, xc = ctx // 4, ctx % 4
 
@@ -74,7 +76,7 @@
         load(wo_in.at[pl.ds(pl.multiple_of((tp + j) % 4 * HD, HD), HD), :], wo.at[pl.ds(j * HD, HD), :])
         for j in range(4)
     ]
-    wq_load = load(wq, w_raw)
+    wq_loads = [load(wq, w_raw)]
 
     barrier = pltpu.get_barrier_semaphore()
     for other in (right, left, across, up, down, after, before):
@@ -125,10 +127,12 @@
         f.fwd_r = msg(part(x, 2, 0, CUT), part(x, 6, 0, CUT), right)
         f.fwd_rq = msg(part(x, 2, CUT, MID), part(x, 6, CUT, MID), right)
         f.fwd_l = msg(part(x, 3, MID, TB), part(x, 6, MID, TB), left)
-        f.fwd_z2 = msg(part(x, 2, CUT, TB), part(x, 4, CUT, TB), across)
-        f.fwd_z3 = msg(part(x, 3, CUT, TB), part(x, 5, CUT, TB), across)
+        f.fwd_z2 = msg(part(x, 2, CUT, SIDE), part(x, 4, CUT, SIDE), across)
+        f.fwd_z3 = msg(part(x, 3, CUT, SIDE), part(x, 5, CUT, SIDE), across)
         f.z_r = msg(part(x, 1, 0, CUT), part(x, 4, 0, CUT), right)
         f.z_l = msg(part(x, 1, 0, CUT), part(x, 5, 0, CUT), left)
+        f.z_rq = msg(part(x, 1, SIDE, TB), part(x, 4, SIDE, TB), right)
+        f.z_lq = msg(part(x, 1, SIDE, TB), part(x, 5, SIDE, TB), left)
         f.z_l2 = msg(part(x, 5, 0, CUT), part(x, 7, 0, CUT), left)
         f.far_a = msg(part(x, 6, CUT, MID), part(x, 7, CUT, MID), across)
         f.far_b = msg(part(x, 6, MID, TB), part(x, 7, MID, TB), across)
@@ -163,14 +167,15 @@
             at = [sum(sizes[:i]) for i in range(len(sizes))]
             return [ref.at[pl.ds(lo, n)] for lo, n in zip(at, sizes)]
 
-        f.zb6, f.zb2, f.zb3, f.z0a, f.z0b = cuts(rz, LOW, LOW, LOW, CUT, LOW)
-        f.la5, f.la1, f.l3, f.l0a, f.l0b = cuts(rl, CUT, CUT, TB - MID, CUT, LOW)
-        f.ra1, f.r2a, f.r2q, f.r0a, f.r0b = cuts(rr, CUT, CUT, MID - CUT, CUT, LOW)
+        f.zb6, f.zb2, f.zb3, f.z0a, f.z0b = cuts(rz, LOW, SIDE - CUT, SIDE - CUT, CUT, LOW)
+        f.la5, f.la1, f.l3, f.l0a, f.l0b, f.lb1 = cuts(rl, CUT, CUT, TB - MID, CUT, LOW, TB - SIDE)
+        f.ra1, f.r2a, f.r2q, f.r0a, f.r0b, f.rb1 = cuts(rr, CUT, CUT, MID - CUT, CUT, LOW, TB - SIDE)
         f.t7r, f.t7z = msg(part(xs, 7, 0, CUT), f.la5, right), msg(part(xs, 7, CUT, TB), f.zb6, across)
         f.t6l, f.t6q = msg(part(xs, 6, 0, CUT), f.r2a, left), msg(part(xs, 6, CUT, MID), f.r2q, left)
         f.t6r = msg(part(xs, 6, MID, TB), f.l3, right)
-        f.t5r, f.t5z = msg(part(xs, 5, 0, CUT), f.la1, right), msg(part(xs, 5, CUT, TB), f.zb3, across)
-        f.t4l, f.t4z = msg(part(xs, 4, 0, CUT), f.ra1, left), msg(part(xs, 4, CUT, TB), f.zb2, across)
+        f.t5r, f.t5z = msg(part(xs, 5, 0, CUT), f.la1, right), msg(part(xs, 5, CUT, SIDE), f.zb3, across)
+        f.t4l, f.t4z = msg(part(xs, 4, 0, CUT), f.ra1, left), msg(part(xs, 4, CUT, SIDE), f.zb2, across)
+        f.t5q, f.t4q = msg(part(xs, 5, SIDE, TB), f.lb1, right), msg(part(xs, 4, SIDE, TB), f.rb1, left)
         f.t3a, f.t3b = msg(part(xs, 3, 0, CUT), f.l0a, right), msg(part(xs, 3, CUT, TB), f.l0b, right)
         f.t2a, f.t2b = msg(part(xs, 2, 0, CUT), f.r0a, left), msg(part(xs, 2, CUT, TB), f.r0b, left)
         f.t1a, f.t1b = msg(part(xs, 1, 0, CUT), f.z0a, across), msg(part(xs, 1, CUT, TB), f.z0b, across)
@@ -193,41 +198,33 @@
             copy.start()
             pending.append((copy, slot))
 
+    seen = set()
+
     def got(*messages):
         for message in messages:
-            message.copy(0).wait_recv()
-
-    def send_own(f):
-        start(f.own_z[0], f.own_r[1], f.own_l[1], f.own_z[1], f.own_r[0], f.own_l[0])
-
-    def pass_low(f):
-        got(f.own_r[1], f.own_l[1])
-        start(f.fwd_z2, f.fwd_z3, f.fwd_rq, f.fwd_l)
-        got(f.own_z[0])
-        start(f.z_l, f.z_r)
-
-    def pass_high(f):
-        got(f.own_r[0])
-        start(f.fwd_r)
-
-    def pass_far_low(f):
-        got(f.fwd_l)
-        start(f.far_b)
-        got(f.fwd_rq)
-        start(f.far_a)
-
-    def pass_far_high(f):
-        got(f.z_l)
-        start(f.z_l2)
-
-    def near_here(f):
-        got(f.own_z[1], f.own_l[0])
-
-    def diagonal_here(f):
-        got(f.z_r, f.fwd_z2)
-
-    def far_here(f):
-        got(f.fwd_z3, f.fwd_r, f.z_l2, f.far_a, f.far_b)
+            if message.k not in seen:
+                seen.add(message.k)
+                message.copy(0).wait_recv()
+
+    def need(copies):
+        while copies:
+            copies.pop().wait()
+
+    def here(f, block):
+        s, half = block
+        return {
+            (0, 0): (), (0, 1): (), (1, 0): (f.own_z[0],), (1, 1): (f.own_z[1],), (2, 0): (f.own_r[0],),
+            (2, 1): (f.own_r[1],), (3, 0): (f.own_l[0],), (3, 1): (f.own_l[1],), (4, 0): (f.z_r,), (4, 1): (f.fwd_z2, f.z_rq),
+            (5, 0): (f.z_l,), (5, 1): (f.fwd_z3, f.z_lq), (6, 0): (f.fwd_r,), (6, 1): (f.fwd_rq, f.fwd_l), (7, 0): (f.z_l2,),
+            (7, 1): (f.far_a, f.far_b),
+        }[block]
+
+    def pass_on(arrived, *onward):
+        def step():
+            got(*arrived)
+            start(*onward)
+
+        return step
 
     def add_into(dst, lo, n, srcs, cols=None):
         @pl.loop(0, n // 16)
@@ -243,6 +240,11 @@
         return pl.ds(f.groups[g][0] * 64, f.groups[g][1] * 64)
 
     def project(f, g):
+        at, n = f.groups[g]
+        for block in ORDER[at:at + n]:
+            got(*here(f, block))
+        need(own_loads)
+        need(wo_loads)
         r = rows_of(f, g)
 
         @pl.loop(0, 4 * f.w // 256, unroll=min(3, 4 * f.w // 256))
@@ -293,6 +295,8 @@
         return (e * (1.0 / jnp.sum(e, axis=-1, keepdims=True))).astype(BF16)
 
     def saved_probs(quarter):
+        need(sv_loads)
+
         @pl.loop(quarter * 2, quarter * 2 + 2)
         def _(i):
             r = pl.ds(pl.multiple_of(i * 128, 128), 128)
@@ -300,11 +304,13 @@
             probs[r, :] = p
             head_out[r, :] = nn(p, sv[2]).astype(BF16)
 
-    def backward_start():
-        dk[...] = jnp.zeros_like(dk)
-        dv[...] = jnp.zeros_like(dv)
+    begun = []
 
     def backward_rows(g):
+        if not begun:
+            begun.append(g)
+            dk[...] = jnp.zeros_like(dk)
+            dv[...] = jnp.zeros_like(dv)
         r = rows_of(fb, g)
         grad = act_b[r, :]
         delta = jnp.sum(grad.astype(F32) * head_out[r, :].astype(F32), axis=-1, keepdims=True)
@@ -321,10 +327,6 @@
         got(fb.queries[1][g])
         start(fb.queries[3][g])
 
-    def queries_here(*groups):
-        for g in groups:
-            got(fb.queries[2][g], fb.queries[3][g])
-
     def backward_end():
         grads[:, pl.ds(HD, HD)] = (dk[...] * scale).astype(BF16)
         grads[:, pl.ds(2 * HD, HD)] = dv[...].astype(BF16)
@@ -351,6 +353,7 @@
         start(f.results[3][g])
 
     def order_weights():
+        need(wq_loads)
         row, col = lax.broadcasted_iota(jnp.int32, (256, 256), 0), lax.broadcasted_iota(jnp.int32, (256, 256), 1)
         pick = jnp.where(col == row % 64 * 4 + (row // 64 + tp) % 4, 1.0, 0.0).astype(BF16)
         for c in range(3):
@@ -365,64 +368,47 @@
                             o[j * 64:j * 64 + 64, k * HD:k * HD + HD]
                         )
 
+    turned = []
+
+    def turn_weights(c):
+        if not turned:
+            turned.append(c)
+            row_id, col_id = (lax.broadcasted_iota(jnp.int32, (512, 512), k) for k in (0, 1))
+            pick[...] = jnp.where(row_id == col_id % 128 * 4 + (col_id // 128 + tp) % 4, 1.0, 0.0).astype(BF16)
+
+        @pl.loop(0, 12, unroll=3)
+        def _(i):
+            o = tn(w_raw[pl.ds(pl.multiple_of((c * 12 + i) * 512, 512), 512), :], pick[...]).astype(BF16)
+            for j in range(4):
+                wpt[pl.ds(j * 384 + c * HD, HD), pl.ds(pl.multiple_of(i * 128, 128), 128)] = o[:, j * HD:j * HD + HD]
+
     def project_back(f, g):
         got(f.results[2][g], f.results[3][g])
+        if f is fb:
+            at, n = RESULTS[g]
+            for k, (first, number) in enumerate(fb.groups):
+                if first < at + n and at < first + number:
+                    got(fb.queries[2][k], fb.queries[3][k])
         r = pl.ds(RESULTS[g][0] * 64, RESULTS[g][1] * 64)
 
         @pl.loop(0, 6, unroll=3)
         def _(n):
             c = pl.ds(pl.multiple_of(n * 256, 256), 256)
-            p = nn(f.heads[r, :], wo[:, c]) if f is ff else nt(f.heads[r, :], wp[c, :])
+            p = nn(f.heads[r, :], wo[:, c]) if f is ff else nn(f.heads[r, :], wpt[:, c])
             f.xs[r, c] = p.astype(BF16)
 
-    def back_6(f):
-        project_back(f, 6)
-        start(f.t7z, f.t7r)
-
-    def back_5(f):
-        project_back(f, 5)
-        start(f.t6l, f.t5z)
-
-    def back_4(f):
-        project_back(f, 4)
-        start(f.t4l, f.t4z)
-
-    def add_6(f):
-        got(f.t7z)
-        add_into(f.xs, row(6, CUT), LOW, [f.zb6])
-        start(f.t6q, f.t6r)
-
-    def add_5(f):
-        got(f.t7r)
-        add_into(f.xs, row(5, 0), CUT, [f.la5])
-        start(f.t5r)
-
-    def back_3(f):
-        project_back(f, 3)
-        start(f.t1b)
-
-    def back_2(f):
-        project_back(f, 2)
-        start(f.t3a)
-        got(f.t6l)
-        add_into(f.xs, row(2, 0), CUT, [f.r2a])
-        start(f.t2a)
-
-    def add_1(f):
-        got(f.t5r, f.t4l)
-        add_into(f.xs, row(1, 0), CUT, [f.la1, f.ra1])
-        start(f.t1a)
-
-    def back_1(f):
-        project_back(f, 1)
-        got(f.t5z, f.t6r)
-        add_into(f.xs, row(3, CUT), LOW, [f.zb3])
-        add_into(f.xs, row(3, MID), TB - MID, [f.l3])
-        start(f.t3b)
-        got(f.t4z, f.t6q)
-        add_into(f.xs, row(2, CUT), LOW, [f.zb2])
-        add_into(f.xs, row(2, CUT), MID - CUT, [f.r2q])
-        start(f.t2b)
+    def back(f, g):
+        project_back(f, g)
+        start(*{6: (f.t7z, f.t7r), 5: (f.t5z, f.t6l, f.t5q), 4: (f.t4z, f.t4l, f.t4q), 2: (f.t3a,)}.get(g, ()))
+
+    def combine(f, arrived, adds, *onward):
+        def step():
+            got(*arrived)
+            for at, n, srcs in adds:
+                add_into(f.xs, at, n, srcs)
+            start(*onward)
+
+        return step
 
     def finish(f, lo, n, srcs, hop):
         @pl.loop(0, n // 16)
@@ -444,140 +430,175 @@
         got(f.t3b, f.t2b, f.t1b)
         finish(f, CUT, LOW, (f.l0b, f.r0b, f.z0b), f.hops[1])
 
-    send_own(ff)
+    for f in flows:
+        f.do = types.SimpleNamespace(
+            own1=pass_on((), f.own_z[0], f.own_r[1], f.own_l[1]),
+            own2=pass_on((), f.own_z[1], f.own_r[0], f.own_l[0]),
+            pz2=pass_on((f.own_r[1],), f.fwd_z2, f.fwd_rq),
+            pz3=pass_on((f.own_l[1],), f.fwd_z3, f.fwd_l),
+            pzl=pass_on((f.own_z[0],), f.z_l, f.z_r),
+            pzs=pass_on((f.own_z[1],), f.z_rq, f.z_lq),
+            pr=pass_on((f.own_r[0],), f.fwd_r),
+            pfb=pass_on((f.fwd_l,), f.far_b),
+            pfa=pass_on((f.fwd_rq,), f.far_a),
+            pl2=pass_on((f.z_l,), f.z_l2),
+            a6=combine(f, (f.t7z,), ((row(6, CUT), LOW, [f.zb6]),), f.t6q, f.t6r),
+            a5=combine(f, (f.t7r,), ((row(5, 0), CUT, [f.la5]),), f.t5r),
+            a2=combine(f, (f.t6l,), ((row(2, 0), CUT, [f.r2a]),), f.t2a),
+            a1=combine(f, (f.t5r, f.t4l), ((row(1, 0), CUT, [f.la1, f.ra1]),), f.t1a),
+            a1b=combine(f, (f.t5q, f.t4q), ((row(1, SIDE), TB - SIDE, [f.lb1, f.rb1]),), f.t1b),
+            a3b=combine(
+                f, (f.t5z, f.t6r), ((row(3, CUT), SIDE - CUT, [f.zb3]), (row(3, MID), TB - MID, [f.l3])), f.t3b
+            ),
+            a2b=combine(
+                f, (f.t4z, f.t6q), ((row(2, CUT), SIDE - CUT, [f.zb2]), (row(2, CUT), MID - CUT, [f.r2q])), f.t2b
+            ),
+            finA=lambda f=f: finish_high(f),
+            finB=lambda f=f: finish_low(f),
+            proj=[functools.partial(project, f, g) for g in range(len(f.groups))],
+            two=[functools.partial(sum_two, f, g) for g in range(len(f.groups))],
+            total=[functools.partial(sum_all, f, g) for g in range(len(f.groups))],
+            on=[functools.partial(heads_on, f, g) for g in range(len(RESULTS))],
+            back=[functools.partial(back, f, g) for g in range(len(RESULTS))],
+        )
+    fwd, bwd = ff.do, fb.do
+
+    fwd.own1()
+    fwd.own2()
+    order_weights()
+    fwd.proj[0]()
+    fwd.pzl()
+    fwd.pz3()
+    fwd.proj[1]()
+    bwd.proj[0]()
+    fwd.pz2()
+    fwd.two[0]()
+    fwd.proj[2]()
+    fwd.pzs()
+    fwd.two[1]()
+    fwd.proj[4]()
+    fwd.pr()
     make_bias()
-    wq_load.wait()
-    order_weights()
-    for copy in own_loads + wo_loads:
-        copy.wait()
-    project(ff, 0)
-    pass_low(ff)
-    project(ff, 1)
-    sum_two(ff, 0)
-    pass_high(ff)
-    near_here(ff)
-    project(ff, 2)
-    pass_far_low(ff)
-    sum_two(ff, 1)
-    sum_all(ff, 0)
-    for copy in sv_loads:
-        copy.wait()
+    fwd.pl2()
+    fwd.pfb()
+    fwd.pfa()
+    fwd.two[2]()
+    bwd.own1()
+    saved_probs(2)
+    bwd.own2()
+    fwd.proj[3]()
+    fwd.two[4]()
+    fwd.total[0]()
+    turn_weights(0)
+    fwd.total[1]()
+    fwd.proj[6]()
+    fwd.proj[5]()
+    fwd.two[3]()
+    fwd.total[2]()
+    saved_probs(1)
+    bwd.proj[1]()
+    bwd.pz2()
+    fwd.two[6]()
+    fwd.total[4]()
+    bwd.pzl()
+    bwd.pz3()
+    fwd.two[5]()
+    turn_weights(2)
+    bwd.pzs()
+    saved_probs(3)
+    bwd.proj[2]()
+    fwd.total[6]()
+    bwd.two[1]()
     saved_probs(0)
-    pass_far_high(ff)
-    send_own(fb)
-    sum_two(ff, 2)
-    got(ff.fwd_z2)
-    project(ff, 3)
-    got(ff.z_r)
-    project(ff, 4)
-    sum_all(ff, 1)
-    sum_two(ff, 3)
-    got(ff.fwd_z3, ff.fwd_r)
-    project(ff, 5)
-    sum_two(ff, 4)
-    got(ff.z_l2, ff.far_a, ff.far_b)
-    project(ff, 6)
-    sum_all(ff, 2)
-    pass_low(fb)
-    sum_two(ff, 5)
-    project(fb, 0)
-    project(fb, 1)
-    sum_two(ff, 6)
-    sum_all(ff, 3)
-    saved_probs(1)
-    pass_high(fb)
-    near_here(fb)
-    project(fb, 2)
-    pass_far_low(fb)
-    sum_all(ff, 4)
-    sum_two(fb, 0)
-    saved_probs(2)
-    sum_all(ff, 5)
-    sum_two(fb, 1)
-    sum_all(ff, 6)
+    bwd.pfa()
+    fwd.total[3]()
+    bwd.two[0]()
+    fwd.total[5]()
     forward_head(6)
-    pass_far_high(fb)
+    bwd.pr()
+    bwd.two[2]()
+    bwd.pl2()
+    forward_head(4)
+    bwd.pfb()
+    forward_head(3)
     forward_head(5)
-    sum_two(fb, 2)
-    forward_head(4)
-    heads_on(ff, 6)
-    diagonal_here(fb)
-    project(fb, 3)
-    forward_head(3)
+    fwd.on[6]()
+    bwd.proj[3]()
+    forward_head(1)
+    fwd.on[4]()
     forward_head(2)
-    heads_on(ff, 5)
-    sum_two(fb, 3)
-    forward_head(1)
+    bwd.proj[4]()
+    fwd.on[5]()
+    fwd.back[6]()
+    bwd.two[3]()
+    bwd.total[2]()
+    bwd.total[0]()
     forward_head(0)
-    back_6(ff)
-    far_here(fb)
-    project(fb, 4)
-    heads_on(ff, 4)
-    sum_all(fb, 0)
-    sum_all(fb, 1)
-    back_5(ff)
-    sum_two(fb, 4)
-    saved_probs(3)
-    backward_start()
+    fwd.on[3]()
+    bwd.total[1]()
+    backward_rows(2)
+    fwd.back[4]()
+    bwd.two[4]()
+    fwd.back[5]()
+    fwd.on[1]()
     backward_rows(0)
     backward_rows(1)
-    heads_on(ff, 3)
-    heads_on(ff, 2)
-    sum_all(fb, 2)
-    backward_rows(2)
-    back_4(ff)
-    add_6(ff)
-    add_5(ff)
-    sum_all(fb, 3)
+    bwd.total[3]()
+    fwd.a5()
+    fwd.on[2]()
     backward_rows(3)
-    sum_all(fb, 4)
+    bwd.total[4]()
     backward_rows(4)
     backward_end()
+    fwd.back[1]()
+    fwd.back[3]()
+    fwd.a6()
     heads_out(fb, 6)
+    fwd.a1b()
     heads_out(fb, 5)
-    heads_on(ff, 1)
-    heads_on(ff, 0)
+    turn_weights(1)
+    fwd.back[2]()
+    queries_on(4)
+    fwd.a2()
+    bwd.on[6]()
+    heads_out(fb, 4)
+    fwd.a1()
+    fwd.a2b()
+    fwd.a3b()
+    bwd.on[5]()
+    queries_on(3)
+    bwd.back[6]()
+    fwd.on[0]()
+    bwd.on[4]()
+    queries_on(2)
+    heads_out(fb, 2)
+    heads_out(fb, 3)
+    bwd.back[5]()
+    fwd.back[0]()
+    heads_out(fb, 0)
+    fwd.finA()
+    bwd.back[4]()
+    heads_out(fb, 1)
+    bwd.a5()
+    queries_on(1)
+    bwd.on[2]()
+    bwd.on[3]()
+    bwd.a6()
+    fwd.finB()
+    bwd.on[1]()
+    bwd.back[2]()
+    bwd.a1()
+    bwd.a2()
+    bwd.back[3]()
     queries_on(0)
-    queries_on(1)
-    queries_on(2)
-    back_3(ff)
-    queries_on(3)
-    queries_on(4)
-    heads_on(fb, 6)
-    heads_out(fb, 4)
-    back_2(ff)
-    add_1(ff)
-    heads_on(fb, 5)
-    back_1(ff)
-    heads_out(fb, 3)
-    heads_out(fb, 2)
-    queries_here(4)
-    back_6(fb)
-    heads_on(fb, 4)
-    heads_out(fb, 1)
-    heads_out(fb, 0)
-    project_back(ff, 0)
-    back_5(fb)
-    finish_high(ff)
-    finish_low(ff)
-    queries_here(3)
-    back_4(fb)
-    add_6(fb)
-    add_5(fb)
-    heads_on(fb, 3)
-    heads_on(fb, 2)
-    queries_here(2)
-    back_3(fb)
-    heads_on(fb, 1)
-    heads_on(fb, 0)
-    queries_here(1)
-    back_2(fb)
-    add_1(fb)
-    back_1(fb)
-    queries_here(0)
-    project_back(fb, 0)
-    finish_high(fb)
-    finish_low(fb)
+    bwd.back[1]()
+    bwd.a1b()
+    bwd.on[0]()
+    bwd.a3b()
+    bwd.a2b()
+    bwd.back[0]()
+    bwd.finA()
+    bwd.finB()
     got(*fb.hops, *ff.hops)
     drain(len(pending))
     assert count[0] == N_SEMS, count
@@ -606,7 +627,8 @@
             vmem(16, 8, T, dtype=F32), vmem(T, T), vmem(T, HD),
             *pair(T, 512, 1536), *pair(512, 128, 384), *pair(512, 128, 384), *pair(T, 128, 384), *pair(T, 128, 384),
             *pair(T, 128, 384), vmem(T, HD, dtype=F32), vmem(T, HD, dtype=F32), vmem(T, 512), vmem(T, 1536),
-            *pair(T, W, W), *pair(TB + 3 * LOW, W, W), *pair(TB + 2 * CUT + TB - MID, W, W), *pair(TB + CUT + MID, W, W), *pair(TB, W, W),
+            *pair(T, W, W), *pair(TB + LOW + 2 * (SIDE - CUT), W, W), *pair(2 * TB + 2 * CUT - MID + TB - SIDE, W, W),
+            *pair(TB + CUT + MID + TB - SIDE, W, W), *pair(TB, W, W), vmem(512, 512), vmem(W, W),
             pltpu.SemaphoreType.DMA((24,)), pltpu.SemaphoreType.DMA((N_SENT,)), pltpu.SemaphoreType.DMA((N_SEMS,)),
         ],
         compiler_params=pltpu.CompilerParams(

time: 122 us -> 112 us (0.918)
  the two profiles are of different devices: /device:TPU:65 before, /device:TPU:33 now
where the time goes in v4:
time: 112 us
  Pallas kernels  111 us (99%)
    pallas_call x1, Pallas kernels, per_device(): pl.pallas_call(kernel, out_shape=[jax.ShapeDtypeStruct((TB, W), BF16)] *...  109 us

profile of v4, /device:TPU:33, one launch (start us, length us, event | category | flops | bytes accessed | tf_op | source)
XLA Modules:
  0.0 111.9 jit_solution(6640829575729536058)
XLA Ops:
  0.6 109.2 %shard_map.77 = (bf16[128,1536]{1,0:T(8,128)(2,1)}, bf16[128,1536]{1,0:T(8,128)(2,1)}) custom-call(bf16[128,1536]{1,0:T(8,128)(2,1)} %bitcast.13, bf16[128,1536]{1,0:T(8,128)(2,1)} %bitcast.14, bf16[18432,128]{1,0:T(8,128)(2,1)} %bitcast.10, bf16[512,1536]{1,0:T(8,128)(2,1)} %bitcast.11, bf16[3,1024,128]{2,1,0:T(8,128)(2,1)} %bitcast.12, s32[3,1,16]{2,1,0:T(1,128)} %bitcast.17), custom_call_target="tpu_custom_call" | custom-call | flops 16000000000 | bytes 10000000 | tf_op jit(solution)/shard_map/pallas_call | solution.py:620
  109.9 2.0 %shard_map.78 = (bf16[128,1536]{1,0:T(8,128)(2,1)}, bf16[128,1536]{1,0:T(8,128)(2,1)}) custom-call(bf16[128,1536]{1,0:T(8,128)(2,1)} %get-tuple-element.6.a, bf16[128,1536]{1,0:T(8,128)(2,1)} %get-tuple-element.7.b), custom_call_target="tpu_custom_call" | custom-call | tf_op jit(solution)/shard_map/pallas_call | solution.py:647

commit v5 on v4

--- a/solution.py
+++ b/solution.py
@@ -227,7 +227,7 @@
         return step
 
     def add_into(dst, lo, n, srcs, cols=None):
-        @pl.loop(0, n // 16)
+        @pl.loop(0, n // 16, unroll=n // 16 if n <= 64 else 1)
         def _(i):
             r = pl.ds(lo + pl.multiple_of(i * 16, 16), 16)
             c = slice(None) if cols is None else cols
@@ -247,7 +247,7 @@
         need(wo_loads)
         r = rows_of(f, g)
 
-        @pl.loop(0, 4 * f.w // 256, unroll=min(3, 4 * f.w // 256))
+        @pl.loop(0, 4 * f.w // 256, unroll=4 * f.w // 256)
         def _(n):
             c = pl.ds(pl.multiple_of(n * 256, 256), 256)
             p = nn(f.x[r, :], wp[:, c]) if f is ff else nt(f.x[r, :], wo[c, :])
@@ -357,7 +357,7 @@
         row, col = lax.broadcasted_iota(jnp.int32, (256, 256), 0), lax.broadcasted_iota(jnp.int32, (256, 256), 1)
         pick = jnp.where(col == row % 64 * 4 + (row // 64 + tp) % 4, 1.0, 0.0).astype(BF16)
         for c in range(3):
-            @pl.loop(0, 12, unroll=4)
+            @pl.loop(0, 12, unroll=6)
             def _(i):
                 a = w_raw[pl.ds(pl.multiple_of((c * 24 + i * 2) * 256, 256), 256), :]
                 b = w_raw[pl.ds(pl.multiple_of((c * 24 + i * 2 + 1) * 256, 256), 256), :]
@@ -391,7 +391,7 @@
                     got(fb.queries[2][k], fb.queries[3][k])
         r = pl.ds(RESULTS[g][0] * 64, RESULTS[g][1] * 64)
 
-        @pl.loop(0, 6, unroll=3)
+        @pl.loop(0, 6, unroll=6)
         def _(n):
             c = pl.ds(pl.multiple_of(n * 256, 256), 256)
             p = nn(f.heads[r, :], wo[:, c]) if f is ff else nn(f.heads[r, :], wpt[:, c])
@@ -411,7 +411,7 @@
         return step
 
     def finish(f, lo, n, srcs, hop):
-        @pl.loop(0, n // 16)
+        @pl.loop(0, n // 16, unroll=n // 16 if n <= 64 else 1)
         def _(i):
             at = pl.multiple_of(i * 16, 16)
             r = pl.ds(lo + at, 16)

time: 112 us -> 111 us (level)
  the two profiles are of different devices: /device:TPU:33 before, /device:TPU:65 now
where the time goes in v5:
time: 111 us; the launch traced here: 110 us
  Pallas kernels  109 us (98%)
    pallas_call x1, Pallas kernels, per_device(): pl.pallas_call(kernel, out_shape=[jax.ShapeDtypeStruct((TB, W), BF16)] *...  107 us

profile of v5, /device:TPU:65, one launch (start us, length us, event | category | flops | bytes accessed | tf_op | source)
XLA Modules:
  0.0 109.6 jit_solution(5605939453472766976)
XLA Ops:
  0.6 107.0 %shard_map.77 = (bf16[128,1536]{1,0:T(8,128)(2,1)}, bf16[128,1536]{1,0:T(8,128)(2,1)}) custom-call(bf16[128,1536]{1,0:T(8,128)(2,1)} %bitcast.13, bf16[128,1536]{1,0:T(8,128)(2,1)} %bitcast.14, bf16[18432,128]{1,0:T(8,128)(2,1)} %bitcast.10, bf16[512,1536]{1,0:T(8,128)(2,1)} %bitcast.11, bf16[3,1024,128]{2,1,0:T(8,128)(2,1)} %bitcast.12, s32[3,1,16]{2,1,0:T(1,128)} %bitcast.17), custom_call_target="tpu_custom_call" | custom-call | flops 16000000000 | bytes 10000000 | tf_op jit(solution)/shard_map/pallas_call | solution.py:620
  107.6 2.0 %shard_map.78 = (bf16[128,1536]{1,0:T(8,128)(2,1)}, bf16[128,1536]{1,0:T(8,128)(2,1)}) custom-call(bf16[128,1536]{1,0:T(8,128)(2,1)} %get-tuple-element.6.a, bf16[128,1536]{1,0:T(8,128)(2,1)} %get-tuple-element.7.b), custom_call_target="tpu_custom_call" | custom-call | tf_op jit(solution)/shard_map/pallas_call | solution.py:647
